TPU v7x, 32 devices: a whole 2x2x4 slice. The times are simulated.
32 devices in a mesh: ctx: 4 (over z), ep: 8 (over y, x, core).
Axes of the slice: x: 2, y: 2, z: 4, core: 2. Of those that a mesh axis runs over, the one named last changes fastest.
Arguments:
- query_act: bfloat16 [512, 2048], P('ctx', 'ep'), may hold values from -6 to 6
- key_act: bfloat16 [512, 2048], P('ctx', 'ep'), may hold values from -6 to 6
- value_act: bfloat16 [512, 2048], P('ctx', 'ep'), may hold values from -6 to 6
- state_init: float32 [16, 128, 128], P('ep'), may hold values from -128 to 128
- head_gain: float32 [2048], P('ep'), may hold values from 0.25 to 1.75
- out_weight: bfloat16 [2048, 3072], P('ctx', 'ep'), may hold values from -0.125 to 0.125
- stream_in: bfloat16 [512, 3072], P('ctx', 'ep'), may hold values from -150 to 150
- model_gain: float32 [3072], replicated, may hold values from 0.25 to 1.75
- expert_ids: int32 [512, 2], P('ctx'), may hold values from 0 to 3, as said below
- expert_slots: int32 [512, 2], P('ctx'), may hold values from 0 to 79, as said below
- route_gates: float32 [512, 2], P('ctx'), may hold values from 0.2 to 1
- gate_weight: bfloat16 [8, 3072, 3072], P('ep', 'ctx'), may hold values from -0.109375 to 0.109375
- up_weight: bfloat16 [8, 3072, 3072], P('ep', 'ctx'), may hold values from -0.109375 to 0.109375
- down_weight: bfloat16 [8, 3072, 3072], P('ep', 'ctx'), may hold values from -0.078125 to 0.078125
- out_grad: bfloat16 [512, 3072], P('ctx', 'ep'), may hold values from -6 to 6
Outputs:
- layer_out: bfloat16 [512, 3072], P('ctx', 'ep')
- grad_query: bfloat16 [512, 2048], P('ctx', 'ep')
- grad_key: bfloat16 [512, 2048], P('ctx', 'ep')
- grad_value: bfloat16 [512, 2048], P('ctx', 'ep')
- grad_state: float32 [16, 128, 128], P('ep')
- grad_stream: bfloat16 [512, 3072], P('ctx', 'ep')
Inputs may be any that keep to these rules, and one draw needn't show every extreme that they name: `expert_ids`: within each block of 128 tokens a token's two experts differ; the tokens naming expert e hold the slots 0 to n - 1 of e once each, n being their number; no expert is named by more than 80 tokens of a block, and in every block some expert by exactly 80. `expert_slots`: see expert_ids.
All inputs are finite; a program needn't handle non-finite values.
Results may differ from a plain program's by a relative error of at most 0.02.
Values may be sent and summed in bfloat16 or wider, within the bound.
A program may use at most 64 MiB of HBM per device.

v0:
```python
import jax
import jax.numpy as jnp
from jax import lax
from jax.sharding import PartitionSpec as P


def carried_in(value, axis, join, neutral, backward):
    count = lax.axis_size(axis)
    place = lax.axis_index(axis)
    ahead = count - 1 - place if backward else place
    gathered = lax.all_gather(value.astype(jnp.bfloat16), axis)
    state = jnp.zeros_like(value) + jnp.asarray(neutral, value.dtype)

    def one(turn, state):
        source = count - 1 - turn if backward else turn
        return join(state, lax.dynamic_index_in_dim(gathered, source, 0, False).astype(value.dtype))

    return lax.fori_loop(0, ahead, one, state)


def head_normalize(attended, gain):
    factor = lax.rsqrt(jnp.mean(attended * attended, -1, keepdims=True) + 1e-06)
    return attended * factor * gain


def add_states(earlier, later_one):
    return earlier + later_one


def contract_last(left, right):
    return lax.dot_general(
        left, right, (((1,), (1,)), ((), ())), preferred_element_type=jnp.float32
    )


def local(
    query_act,
    key_act,
    value_act,
    state_init,
    head_gain,
    out_weight,
    stream_in,
    model_gain,
    expert_ids,
    expert_slots,
    route_gates,
    gate_weight,
    up_weight,
    down_weight,
    out_grad,
):
    f32 = jnp.float32
    high = lax.Precision.HIGHEST
    ep_count = lax.axis_size("ep")
    expert_count = ep_count // 2
    my_ep = lax.axis_index("ep")
    tokens_here = query_act.shape[0]
    head_count = state_init.shape[0]
    head_size = state_init.shape[1]
    model_width = model_gain.shape[0]
    columns = stream_in.shape[1]
    capacity = 5 * tokens_here // (2 * expert_count)
    query3 = query_act.reshape(tokens_here, head_count, head_size)
    key3 = key_act.reshape(tokens_here, head_count, head_size)
    value3 = value_act.reshape(tokens_here, head_count, head_size)
    kv_own = jnp.einsum("thd,the->hde", key3, value3, preferred_element_type=f32)
    zero_state = jnp.zeros_like(kv_own)
    before = carried_in(kv_own, "ctx", add_states, zero_state, False)
    prefix = state_init + before
    causal = jnp.arange(tokens_here)[:, None] >= jnp.arange(tokens_here)[None, :]
    scores = jnp.einsum("thd,shd->hts", query3, key3, preferred_element_type=f32)
    scores_bf = jnp.where(causal[None], scores, 0.0).astype(jnp.bfloat16)
    inside = jnp.einsum("hts,she->the", scores_bf, value3, preferred_element_type=f32)
    from_state = jnp.einsum("thd,hde->the", query3.astype(f32), prefix, precision=high)
    attended = from_state + inside
    gain_heads = head_gain.reshape(head_count, head_size)
    normed_heads = (
        head_normalize(attended, gain_heads)
        .astype(jnp.bfloat16)
        .reshape(tokens_here, head_count * head_size)
    )
    w_cols = lax.all_gather(out_weight, "ctx", axis=0, tiled=True)
    attn_proj = jnp.dot(
        lax.all_gather(normed_heads, "ep", axis=1, tiled=True), w_cols, preferred_element_type=f32
    )
    stream = (stream_in.astype(f32) + attn_proj).astype(jnp.bfloat16)
    stream_f = stream.astype(f32)
    gain_cols = lax.dynamic_slice_in_dim(model_gain, my_ep * columns, columns, 0)
    dest_expert = jnp.arange(ep_count) % expert_count
    slot_iota = jnp.arange(capacity)
    hits = (expert_ids[:, :, None, None] == dest_expert[None, None, :, None]) & (
        expert_slots[:, :, None, None] == slot_iota[None, None, None, :]
    )
    hits_f = hits.astype(f32)
    dest_picks = jnp.sum(hits_f, 1).reshape(tokens_here, ep_count * capacity)
    dest_weights = jnp.sum(hits_f * route_gates[:, :, None, None], 1).reshape(
        tokens_here, ep_count * capacity
    )
    whole_rows = lax.all_gather(stream, "ep", axis=1, tiled=True).astype(f32)
    row_scale = lax.rsqrt(jnp.mean(whole_rows * whole_rows, -1, keepdims=True) + 1e-05)
    model_in = (whole_rows * row_scale * model_gain).astype(jnp.bfloat16)
    own_select = lax.dynamic_slice_in_dim(dest_picks, my_ep * capacity, capacity, 1).T.astype(
        jnp.bfloat16
    )
    expert_in = jnp.dot(own_select, model_in, preferred_element_type=f32).astype(jnp.bfloat16)
    w_gate = gate_weight[0]
    w_up = up_weight[0]
    w_down = down_weight[0]
    hidden_block = w_gate.shape[0]
    portion = lax.all_gather(expert_in, "ctx", axis=0, tiled=True)
    projected = jnp.concatenate([contract_last(portion, w_gate), contract_last(portion, w_up)], 1)
    pre_gate = projected[:, :hidden_block]
    pre_up = projected[:, hidden_block:]
    gate_sig = jax.nn.sigmoid(pre_gate)
    activated = (pre_gate * gate_sig * pre_up).astype(jnp.bfloat16)
    half_out = lax.psum_scatter(
        jnp.dot(activated, w_down, preferred_element_type=f32).astype(jnp.bfloat16),
        "ctx",
        scatter_dimension=0,
        tiled=True,
    )
    returned = lax.all_to_all(half_out, "ep", split_axis=1, concat_axis=0, tiled=True)
    expert_mix = jnp.dot(dest_weights, returned.astype(f32), precision=high)
    layer_out = (stream_f + expert_mix).astype(jnp.bfloat16)
    grad_out = out_grad.astype(f32)
    grad_send = jnp.dot(dest_weights.T, grad_out, precision=high).astype(jnp.bfloat16)
    grad_in = lax.all_to_all(grad_send, "ep", split_axis=0, concat_axis=1, tiled=True)
    grad_act = contract_last(lax.all_gather(grad_in, "ctx", axis=0, tiled=True), w_down)
    grad_gate_pre = (grad_act * pre_up * gate_sig * (1.0 + pre_gate * (1.0 - gate_sig))).astype(
        jnp.bfloat16
    )
    grad_up_pre = (grad_act * pre_gate * gate_sig).astype(jnp.bfloat16)
    grad_half = lax.psum_scatter(
        (
            jnp.dot(grad_gate_pre, w_gate, preferred_element_type=f32)
            + jnp.dot(grad_up_pre, w_up, preferred_element_type=f32)
        ).astype(jnp.bfloat16),
        "ctx",
        scatter_dimension=0,
        tiled=True,
    )
    grad_back = lax.all_to_all(grad_half, "ep", split_axis=1, concat_axis=0, tiled=True)
    grad_model_in = jnp.dot(dest_picks, grad_back.astype(f32), precision=high)
    scaled_grad = grad_model_in * gain_cols
    inner_sum = lax.psum(jnp.sum(stream_f * scaled_grad, -1), "ep")
    grad_stream = (
        grad_out
        + row_scale * scaled_grad
        - stream_f * row_scale**3 * inner_sum[:, None] / model_width
    ).astype(jnp.bfloat16)
    w_rows = lax.all_to_all(w_cols, "ep", split_axis=0, concat_axis=1, tiled=True)
    grad_heads = contract_last(lax.all_gather(grad_stream, "ep", axis=1, tiled=True), w_rows)
    head_pull = jax.vjp(lambda value: head_normalize(value, gain_heads), attended)[1]
    grad_attended = head_pull(grad_heads.reshape(tokens_here, head_count, head_size))[0].astype(
        jnp.bfloat16
    )
    state_part = jnp.einsum("thd,the->hde", query3, grad_attended, preferred_element_type=f32)
    later_sum = carried_in(state_part, "ctx", add_states, zero_state, True)
    state_total = lax.psum(state_part.astype(jnp.bfloat16), "ctx").astype(jnp.float32)
    grad_scores = jnp.einsum("the,she->hts", grad_attended, value3, preferred_element_type=f32)
    grad_masked = jnp.where(causal[None], grad_scores, 0.0).astype(jnp.bfloat16)
    grad_att_f = grad_attended.astype(f32)
    grad_query = jnp.einsum("the,hde->thd", grad_att_f, prefix, precision=high) + jnp.einsum(
        "hts,shd->thd", grad_masked, key3, preferred_element_type=f32
    )
    grad_key = jnp.einsum(
        "the,hde->thd", value3.astype(f32), later_sum, precision=high
    ) + jnp.einsum("hts,thd->shd", grad_masked, query3, preferred_element_type=f32)
    grad_value = jnp.einsum(
        "thd,hde->the", key3.astype(f32), later_sum, precision=high
    ) + jnp.einsum("hts,the->she", scores_bf, grad_attended, preferred_element_type=f32)
    flat_shape = (tokens_here, head_count * head_size)
    return (
        layer_out,
        grad_query.astype(jnp.bfloat16).reshape(flat_shape),
        grad_key.astype(jnp.bfloat16).reshape(flat_shape),
        grad_value.astype(jnp.bfloat16).reshape(flat_shape),
        state_total,
        grad_stream,
    )


def solution(mesh):
    return jax.shard_map(
        local,
        mesh=mesh,
        in_specs=(
            P("ctx", "ep"),
            P("ctx", "ep"),
            P("ctx", "ep"),
            P("ep", None, None),
            P("ep"),
            P("ctx", "ep"),
            P("ctx", "ep"),
            P(),
            P("ctx", None),
            P("ctx", None),
            P("ctx", None),
            P("ep", "ctx", None),
            P("ep", "ctx", None),
            P("ep", "ctx", None),
            P("ctx", "ep"),
        ),
        out_specs=(
            P("ctx", "ep"),
            P("ctx", "ep"),
            P("ctx", "ep"),
            P("ctx", "ep"),
            P("ep", None, None),
            P("ctx", "ep"),
        ),
        check_vma=False,
    )
```

profile of v0, /device:TPU:0, one launch (start us, length us, event | category | flops | bytes accessed | tf_op | source)
XLA Modules:
  0.0 328.7 jit_solution(7615919780394305283)
XLA Ops:
  7.2 0.7 all-gather.6.cloned.1.call-update
  7.9 0.8 broadcast_compare_fusion
  8.7 0.7 iota_compare_fusion
  9.4 0.9 fusion.42
  10.3 2.3 convolution_convert_fusion.1
  12.6 5.2 %all-to-all-start.1 = ((bf16[8,80,384]{2,1,0:T(8,128)(2,1)}), bf16[8,80,384]{2,1,0:T(8,128)(2,1)S(1)}, u32[]{:S(2)}, u32[]{:S(2)}) async-start(bf16[8,80,384]{2,1,0:T(8,128)(2,1)} %bitcast.14), calls=%async_computation.2 | async-start | bytes 983040 | tf_op jit(solution)/shard_map/all_to_all | solution.py:128
  18.1 0.5 copy-done.11
  18.8 16.8 %all-gather = bf16[8,128,128]{2,1,0:T(8,128)(2,1)S(1)} all-gather(bf16[2,128,128]{2,1,0:T(8,128)(2,1)S(1)} %convolution_convert_fusion.3), channel_id=2, replica_groups=mesh['ctx'=4,'ep'=8] {'ctx'}, dimensions={0}, use_global_device_ids=true | all-gather | bytes 327680 | tf_op jit(solution)/shard_map/all_gather | solution.py:11
  35.6 0.9 copy.138
  36.9 0.3 convolution_bitcast_fusion.7
  37.6 10.2 %all_gather.32 = bf16[128,2048]{0,1:T(8,128)(2,1)S(1)} all-gather(bf16[128,256]{0,1:T(8,128)(2,1)S(1)} %bitcast.184), channel_id=1, replica_groups=mesh['ctx'=4,'ep'=8] {'ep'}, dimensions={1}, use_global_device_ids=true | all-gather | bytes 589824 | tf_op jit(solution)/shard_map/all_gather | solution.py:85
  47.8 6.0 %all-gather.6.cloned.1.call-done = bf16[2048,384]{1,0:T(8,128)(2,1)} async-done(((bf16[512,384]{1,0:T(8,128)(2,1)}), bf16[2048,384]{1,0:T(8,128)(2,1)}) %all-gather.6.cloned.1.call-update) | async-done | bytes 1572880 | tf_op jit(solution)/shard_map/all_gather | solution.py:83
  53.8 1.9 fusion.27
  55.7 0.6 copy-done.1
  56.3 10.9 %all_gather.34 = bf16[128,3072]{1,0:T(8,128)(2,1)S(1)} all-gather(bf16[128,384]{1,0:T(8,128)(2,1)S(1)} %fusion.27), channel_id=1, replica_groups=mesh['ctx'=4,'ep'=8] {'ep'}, dimensions={1}, use_global_device_ids=true | all-gather | bytes 884736 | tf_op jit(solution)/shard_map/all_gather | solution.py:100
  67.5 0.6 multiply_multiply_fusion.1
  68.1 1.2 convolution_convert_fusion
  69.4 28.6 %all-gather.10.cloned.1.call-done = bf16[320,3072]{1,0:T(8,128)(2,1)} async-done(((bf16[80,3072]{1,0:T(8,128)(2,1)}), bf16[320,3072]{1,0:T(8,128)(2,1)}) %all-gather.10.cloned.1.call-update) | async-done | bytes 1966096 | tf_op jit(solution)/shard_map/all_gather | solution.py:129
  98.0 4.7 %fusion = f32[320,768]{1,0:T(8,128)S(1)} fusion(bf16[320,3072]{1,0:T(8,128)(2,1)} %all-gather.10.cloned.1.call-done, bf16[1,768,3072]{2,1,0:T(8,128)(2,1)} %param.32), kind=kOutput, calls=%fused_computation.2 | convolution fusion | flops 1509949440 | bytes 7667712 | tf_op jit(solution)/shard_map/dot_general | solution.py:31
  102.7 39.3 %all-gather.8.cloned.1.call-done = bf16[320,3072]{1,0:T(8,128)(2,1)} async-done(((bf16[80,3072]{1,0:T(8,128)(2,1)}), bf16[320,3072]{1,0:T(8,128)(2,1)}) %all-gather.8.cloned.1.call-update) | async-done | bytes 1966096 | tf_op jit(solution)/shard_map/all_gather | solution.py:111
  142.1 4.8 %fusion.10 = f32[320,768]{1,0:T(8,128)S(1)} fusion(bf16[320,3072]{1,0:T(8,128)(2,1)} %all-gather.8.cloned.1.call-done, bf16[1,768,3072]{2,1,0:T(8,128)(2,1)} %param.30), kind=kOutput, calls=%fused_computation.12 | convolution fusion | flops 1509949440 | bytes 7667712 | tf_op jit(solution)/shard_map/dot_general | solution.py:31
  146.9 4.3 %fusion.4 = f32[320,3072]{1,0:T(8,128)S(1)} fusion(bf16[1,768,3072]{2,1,0:T(8,128)(2,1)} %param.31, f32[320,768]{1,0:T(8,128)S(1)} %fusion, f32[320,768]{1,0:T(8,128)S(1)} %fusion.10), kind=kOutput, calls=%fused_computation.6 | convolution fusion | flops 1511424000 | bytes 10616832 | tf_op jit(solution)/shard_map/dot_general | solution.py:137
  151.2 1.7 fusion.6
  153.0 3.2 fusion.15
  156.4 5.4 %fusion.18 = bf16[320,3072]{1,0:T(8,128)(2,1)} fusion(bf16[1,768,3072]{2,1,0:T(8,128)(2,1)} %param.32, f32[320,768]{1,0:T(8,128)S(1)} %fusion.6, f32[320,768]{1,0:T(8,128)S(1)} %fusion.10), kind=kOutput, calls=%fused_computation.16 | convolution fusion | flops 1512407040 | bytes 8650752 | tf_op jit(solution)/shard_map/dot_general | solution.py:118
  161.8 3.7 %all-to-all-start.3 = ((bf16[8,256,384]{2,1,0:T(8,128)(2,1)}), bf16[8,256,384]{2,1,0:T(8,128)(2,1)S(1)}, u32[]{:S(2)}, u32[]{:S(2)}) async-start(bf16[8,256,384]{2,1,0:T(8,128)(2,1)} %bitcast.19), calls=%async_computation.5 | async-start | bytes 3145728 | tf_op jit(solution)/shard_map/all_to_all | solution.py:152
  165.5 31.1 %reduce-scatter.5.cloned.1.call-done = bf16[80,3072]{1,0:T(8,128)(2,1)} async-done(((bf16[320,3072]{1,0:T(8,128)(2,1)}), bf16[80,3072]{1,0:T(8,128)(2,1)}) %reduce-scatter.5.cloned.1.call-update) | async-done | bytes 491536 | tf_op jit(solution)/shard_map/reduce_scatter | solution.py:134
  196.6 1.9 copy.168
  198.5 4.1 %all-to-all-start.2 = ((bf16[80,8,384]{2,0,1:T(8,128)(2,1)}), bf16[80,8,384]{2,0,1:T(8,128)(2,1)}, u32[]{:S(2)}, u32[]{:S(2)}) async-start(bf16[80,8,384]{2,0,1:T(8,128)(2,1)} %bitcast.163), calls=%async_computation.4 | async-start | bytes 983040 | tf_op jit(solution)/shard_map/all_to_all | solution.py:143
  202.6 0.7 dynamic_slice.18
  203.3 0.9 copy.114
  204.2 0.8 dot_general.89
  205.1 34.4 %reduce-scatter.3.cloned.1.call-done = bf16[80,3072]{1,0:T(8,128)(2,1)} async-done(((bf16[320,3072]{1,0:T(8,128)(2,1)}), bf16[80,3072]{1,0:T(8,128)(2,1)}) %reduce-scatter.3.cloned.1.call-update) | async-done | bytes 491536 | tf_op jit(solution)/shard_map/reduce_scatter | solution.py:117
  239.5 1.9 copy.169
  241.4 3.8 %all-to-all-start = ((bf16[80,8,384]{2,0,1:T(8,128)(2,1)}), bf16[80,8,384]{2,0,1:T(8,128)(2,1)S(1)}, u32[]{:S(2)}, u32[]{:S(2)}) async-start(bf16[80,8,384]{2,0,1:T(8,128)(2,1)} %bitcast.164), calls=%async_computation.1 | async-start | bytes 983040 | tf_op jit(solution)/shard_map/all_to_all | solution.py:123
  245.2 1.6 fusion.52
  246.8 14.5 %psum.14 = f32[128]{0:T(128)S(1)} all-reduce(f32[128]{0:T(128)S(1)} %get-tuple-element.141), channel_id=1, replica_groups=mesh['ctx'=4,'ep'=8] {'ep'}, use_global_device_ids=true, to_apply=%region_9.10 | all-reduce | flops 128 | bytes 1024 | tf_op jit(solution)/shard_map/psum | solution.py:146
  261.5 10.9 %all_gather.37 = bf16[128,3072]{1,0:T(8,128)(2,1)S(1)} all-gather(bf16[128,384]{1,0:T(8,128)(2,1)S(1)} %fusion.51), channel_id=1, replica_groups=mesh['ctx'=4,'ep'=8] {'ep'}, dimensions={1}, use_global_device_ids=true | all-gather | bytes 884736 | tf_op jit(solution)/shard_map/all_gather | solution.py:153
  272.4 0.6 multiply_reduce_fusion
  273.9 14.0 %all-gather.1 = bf16[8,128,128]{2,1,0:T(8,128)(2,1)S(1)} all-gather(bf16[2,128,128]{2,1,0:T(8,128)(2,1)S(1)} %copy.120), channel_id=3, replica_groups=mesh['ctx'=4,'ep'=8] {'ctx'}, dimensions={0}, use_global_device_ids=true | all-gather | bytes 327680 | tf_op jit(solution)/shard_map/all_gather | solution.py:11
  288.1 0.2 convolution_bitcast_fusion.3
  288.7 0.3 fusion.54
  289.0 1.2 fusion.26
  290.4 0.7 copy.125
  291.1 0.7 copy.126
  291.9 0.7 copy.127
  292.6 27.7 %all-reduce.2.cloned.1.call-done = bf16[2,128,128]{1,2,0:T(8,128)(2,1)} async-done(((bf16[2,128,128]{1,2,0:T(8,128)(2,1)}), bf16[2,128,128]{1,2,0:T(8,128)(2,1)}) %all-reduce.2.cloned.1.call-update) | async-done | bytes 65552 | tf_op jit(solution)/shard_map/psum | solution.py:160
  320.3 1.6 copy.128
  (125 shorter events, 3.6 us)
Async XLA Ops:
  7.2 11.5 %copy-start = (bf16[128,256]{1,0:T(8,128)(2,1)S(1)}, bf16[128,256]{1,0:T(8,128)(2,1)}, u32[]{:S(2)}) copy-start(bf16[128,256]{1,0:T(8,128)(2,1)} %param.21) | copy-start | bytes 196612
  7.2 10.7 %copy-start.16 = (bf16[128,256]{1,0:T(8,128)(2,1)S(1)}, bf16[128,256]{1,0:T(8,128)(2,1)}, u32[]{:S(2)}) copy-start(bf16[128,256]{1,0:T(8,128)(2,1)} %param.20) | copy-start | bytes 196612
  7.2 10.8 %copy-start.22 = (bf16[128,256]{1,0:T(8,128)(2,1)S(1)}, bf16[128,256]{1,0:T(8,128)(2,1)}, u32[]{:S(2)}) copy-start(bf16[128,256]{1,0:T(8,128)(2,1)} %param.19) | copy-start | bytes 196612
  7.2 46.6 %all-gather.6.cloned.1.call-start = ((), (), s32[]{:S(2)}) async-start(), calls=%async_computation.6 | async-start | bytes 1966080 | tf_op jit(solution)/shard_map/all_gather | solution.py:83
  10.3 57.8 %copy-start.5 = (f32[128,8,80]{0,2,1:T(8,128)}, f32[128,8,80]{0,2,1:T(8,128)S(1)}, u32[]{:S(2)}) copy-start(f32[128,8,80]{0,2,1:T(8,128)S(1)} %get-tuple-element.119) | copy-start | bytes 983044
  12.6 23.0 %all-to-all-start.1 = ((bf16[8,80,384]{2,1,0:T(8,128)(2,1)}), bf16[8,80,384]{2,1,0:T(8,128)(2,1)S(1)}, u32[]{:S(2)}, u32[]{:S(2)}) async-start(bf16[8,80,384]{2,1,0:T(8,128)(2,1)} %bitcast.14), calls=%async_computation.2 | async-start | bytes 983040 | tf_op jit(solution)/shard_map/all_to_all | solution.py:128
  17.8 80.2 %all-gather.10.cloned.1.call-start = ((), (), s32[]{:S(2)}) async-start(), calls=%async_computation.9 | async-start | bytes 2457600 | tf_op jit(solution)/shard_map/all_gather | solution.py:129
  18.1 18.8 %copy-start.9 = (bf16[128,256]{0,1:T(8,128)(2,1)}, bf16[128,256]{0,1:T(8,128)(2,1)S(1)}, u32[]{:S(2)}) copy-start(bf16[128,256]{0,1:T(8,128)(2,1)S(1)} %copy.133) | copy-start | bytes 196612
  18.6 18.0 %copy-start.20 = (f32[2,128,128]{2,1,0:T(8,128)S(1)}, f32[2,128,128]{2,1,0:T(8,128)}, u32[]{:S(2)}) copy-start(f32[2,128,128]{2,1,0:T(8,128)} %param.22) | copy-start | bytes 393220
  36.5 1.0 copy-start.28
  36.5 105.5 %all-gather.8.cloned.1.call-start = ((), (), s32[]{:S(2)}) async-start(), calls=%async_computation.7 | async-start | bytes 2457600 | tf_op jit(solution)/shard_map/all_gather | solution.py:111
  36.6 17.2 %copy-start.21 = (bf16[128,384]{1,0:T(8,128)(2,1)S(1)}, bf16[128,384]{1,0:T(8,128)(2,1)}, u32[]{:S(2)}) copy-start(bf16[128,384]{1,0:T(8,128)(2,1)} %param.25) | copy-start | bytes 294916
  36.9 30.3 %copy-start.18 = (bf16[2,128,128]{2,1,0:T(8,128)(2,1)}, bf16[2,128,128]{2,1,0:T(8,128)(2,1)S(1)}, u32[]{:S(2)}) copy-start(bf16[2,128,128]{2,1,0:T(8,128)(2,1)S(1)} %fusion.31) | copy-start | bytes 196612
  37.4 29.8 %copy-start.3 = (f32[128,2,128]{0,2,1:T(8,128)}, f32[128,2,128]{0,2,1:T(8,128)S(1)}, u32[]{:S(2)}) copy-start(f32[128,2,128]{0,2,1:T(8,128)S(1)} %get-tuple-element.140) | copy-start | bytes 393220
  37.4 29.8 %copy-start.25 = (f32[128,2]{0,1:T(2,128)}, f32[128,2]{0,1:T(2,128)S(1)}, u32[]{:S(2)}) copy-start(f32[128,2]{0,1:T(2,128)S(1)} %get-tuple-element.139) | copy-start | bytes 3076
  37.5 29.8 %copy-start.23 = (f32[128,2]{0,1:T(2,128)}, f32[128,2]{0,1:T(2,128)S(1)}, u32[]{:S(2)}) copy-start(f32[128,2]{0,1:T(2,128)S(1)} %fusion.67) | copy-start | bytes 3076
  47.8 20.2 %copy-start.33 = (f32[3072]{0:T(1024)S(1)}, f32[3072]{0:T(1024)}, u32[]{:S(2)}) copy-start(f32[3072]{0:T(1024)} %param.26) | copy-start | bytes 36868
  68.1 34.6 %copy-start.31 = (f32[128]{0:T(128)}, f32[128]{0:T(128)S(1)}, u32[]{:S(2)}) copy-start(f32[128]{0:T(128)S(1)} %get-tuple-element.138) | copy-start | bytes 1540
  69.3 127.3 %reduce-scatter.5.cloned.1.call-start = ((), (), s32[]{:S(2)}) async-start(), calls=%async_computation.10 | async-start | bytes 2457600 | tf_op jit(solution)/shard_map/reduce_scatter | solution.py:134
  102.7 44.1 %copy-start.35 = (f32[320,768]{1,0:T(8,128)}, f32[320,768]{1,0:T(8,128)S(1)}, u32[]{:S(2)}) copy-start(f32[320,768]{1,0:T(8,128)S(1)} %fusion) | copy-start | bytes 2949124
  142.0 9.1 %slice-start = ((s8[4718592]{0:T(1024)(128)(4,1)}), s8[4194304]{0:T(1024)(128)(4,1)S(1)}, s32[]{:S(2)}) async-start(s8[4718592]{0:T(1024)(128)(4,1)} %bitcast.190), calls=%async_computation.12 | async-start | bytes 8388608
  142.0 10.9 %slice-start.2 = ((s8[4718592]{0:T(1024)(128)(4,1)}), s8[4194304]{0:T(1024)(128)(4,1)S(1)}, s32[]{:S(2)}) async-start(s8[4718592]{0:T(1024)(128)(4,1)} %bitcast.192), calls=%async_computation.14 | async-start | bytes 8388608
  146.9 4.3 %slice-start.1 = ((s8[4718592]{0:T(1024)(128)(4,1)}), s8[524288]{0:T(1024)(128)(4,1)S(1)}, s32[]{:S(2)}) async-start(s8[4718592]{0:T(1024)(128)(4,1)} %bitcast.190), calls=%async_computation.13 | async-start | bytes 1048576
  146.9 4.3 %copy-start.34 = (bf16[320,3072]{1,0:T(8,128)(2,1)S(1)}, bf16[320,3072]{1,0:T(8,128)(2,1)}, u32[]{:S(2)}) copy-start(bf16[320,3072]{1,0:T(8,128)(2,1)} %all-gather.8.cloned.1.call-done) | copy-start | bytes 5898244
  146.9 6.1 %slice-start.3 = ((s8[4718592]{0:T(1024)(128)(4,1)}), s8[524288]{0:T(1024)(128)(4,1)S(1)}, s32[]{:S(2)}) async-start(s8[4718592]{0:T(1024)(128)(4,1)} %bitcast.192), calls=%async_computation.15 | async-start | bytes 1048576
  151.2 1.8 copy-start.36
  156.2 83.3 %reduce-scatter.3.cloned.1.call-start = ((), (), s32[]{:S(2)}) async-start(), calls=%async_computation.8 | async-start | bytes 2457600 | tf_op jit(solution)/shard_map/reduce_scatter | solution.py:117
  161.8 36.7 %all-to-all-start.3 = ((bf16[8,256,384]{2,1,0:T(8,128)(2,1)}), bf16[8,256,384]{2,1,0:T(8,128)(2,1)S(1)}, u32[]{:S(2)}, u32[]{:S(2)}) async-start(bf16[8,256,384]{2,1,0:T(8,128)(2,1)} %bitcast.19), calls=%async_computation.5 | async-start | bytes 3145728 | tf_op jit(solution)/shard_map/all_to_all | solution.py:152
  198.5 42.9 %all-to-all-start.2 = ((bf16[80,8,384]{2,0,1:T(8,128)(2,1)}), bf16[80,8,384]{2,0,1:T(8,128)(2,1)}, u32[]{:S(2)}, u32[]{:S(2)}) async-start(bf16[80,8,384]{2,0,1:T(8,128)(2,1)} %bitcast.163), calls=%async_computation.4 | async-start | bytes 983040 | tf_op jit(solution)/shard_map/all_to_all | solution.py:143
  205.0 40.2 %copy-start.2 = (bf16[128,384]{1,0:T(8,128)(2,1)S(1)}, bf16[128,384]{1,0:T(8,128)(2,1)}, u32[]{:S(2)}) copy-start(bf16[128,384]{1,0:T(8,128)(2,1)} %copy-done.1) | copy-start | bytes 294916
  205.0 40.2 %copy-start.6 = (f32[128,8,80]{0,2,1:T(8,128)S(1)}, f32[128,8,80]{0,2,1:T(8,128)}, u32[]{:S(2)}) copy-start(f32[128,8,80]{0,2,1:T(8,128)} %copy-done.5) | copy-start | bytes 983044
  205.0 40.2 %copy-start.27 = (f32[384]{0:T(512)S(1)}, f32[384]{0:T(512)}, u32[]{:S(2)}) copy-start(f32[384]{0:T(512)} %dynamic_slice.18) | copy-start | bytes 4612
  205.0 56.3 %copy-start.14 = (bf16[128,384]{1,0:T(8,128)(2,1)S(1)}, bf16[128,384]{1,0:T(8,128)(2,1)}, u32[]{:S(2)}) copy-start(bf16[128,384]{1,0:T(8,128)(2,1)} %param.33) | copy-start | bytes 294916
  205.0 56.3 %copy-start.30 = (f32[128]{0:T(128)S(1)}, f32[128]{0:T(128)}, u32[]{:S(2)}) copy-start(f32[128]{0:T(128)} %get-tuple-element.137) | copy-start | bytes 1540
  205.0 56.3 %copy-start.32 = (f32[128]{0:T(128)S(1)}, f32[128]{0:T(128)}, u32[]{:S(2)}) copy-start(f32[128]{0:T(128)} %copy-done.31) | copy-start | bytes 1540
  241.4 31.0 %copy-start.4 = (f32[128,2,128]{0,2,1:T(8,128)S(1)}, f32[128,2,128]{0,2,1:T(8,128)}, u32[]{:S(2)}) copy-start(f32[128,2,128]{0,2,1:T(8,128)} %copy-done.3) | copy-start | bytes 393220
  241.4 31.0 %copy-start.29 = (f32[256]{0:T(256)S(1)}, f32[256]{0:T(256)}, u32[]{:S(2)}) copy-start(f32[256]{0:T(256)} %param.23) | copy-start | bytes 3076
  241.4 47.7 %all-to-all-start = ((bf16[80,8,384]{2,0,1:T(8,128)(2,1)}), bf16[80,8,384]{2,0,1:T(8,128)(2,1)S(1)}, u32[]{:S(2)}, u32[]{:S(2)}) async-start(bf16[80,8,384]{2,0,1:T(8,128)(2,1)} %bitcast.164), calls=%async_computation.1 | async-start | bytes 983040 | tf_op jit(solution)/shard_map/all_to_all | solution.py:123
  261.3 11.7 %copy-start.26 = (f32[128,2]{0,1:T(2,128)S(1)}, f32[128,2]{0,1:T(2,128)}, u32[]{:S(2)}) copy-start(f32[128,2]{0,1:T(2,128)} %copy-done.25) | copy-start | bytes 3076
  261.3 11.7 %copy-start.24 = (f32[128,2]{0,1:T(2,128)S(1)}, f32[128,2]{0,1:T(2,128)}, u32[]{:S(2)}) copy-start(f32[128,2]{0,1:T(2,128)} %copy-done.23) | copy-start | bytes 3076
  261.5 11.8 %copy-start.15 = (bf16[128,384]{1,0:T(8,128)(2,1)}, bf16[128,384]{1,0:T(8,128)(2,1)S(1)}, u32[]{:S(2)}) copy-start(bf16[128,384]{1,0:T(8,128)(2,1)S(1)} %fusion.51) | copy-start | bytes 294916
  261.5 11.6 %copy-start.8 = (f32[2,128,128]{2,1,0:T(8,128)S(1)}, f32[2,128,128]{2,1,0:T(8,128)}, u32[]{:S(2)}) copy-start(f32[2,128,128]{2,1,0:T(8,128)} %copy-done.7) | copy-start | bytes 393220
  272.4 1.1 copy-start.10
  273.0 15.4 %copy-start.12 = (bf16[128,256]{0,1:T(8,128)(2,1)S(1)}, bf16[128,256]{0,1:T(8,128)(2,1)}, u32[]{:S(2)}) copy-start(bf16[128,256]{0,1:T(8,128)(2,1)} %copy-done.11) | copy-start | bytes 196612
  273.3 15.4 %copy-start.17 = (bf16[128,256]{1,0:T(8,128)(2,1)S(1)}, bf16[128,256]{1,0:T(8,128)(2,1)}, u32[]{:S(2)}) copy-start(bf16[128,256]{1,0:T(8,128)(2,1)} %param.20) | copy-start | bytes 196612
  273.7 14.2 %copy-start.13 = (bf16[2,128,128]{1,2,0:T(8,128)(2,1)}, bf16[2,128,128]{1,2,0:T(8,128)(2,1)S(1)}, u32[]{:S(2)}) copy-start(bf16[2,128,128]{1,2,0:T(8,128)(2,1)S(1)} %fusion.36) | copy-start | bytes 196612
  273.9 46.4 %all-reduce.2.cloned.1.call-start = ((), (), s32[]{:S(2)}) async-start(), calls=%async_computation.11 | async-start | bytes 131072 | tf_op jit(solution)/shard_map/psum | solution.py:160
  288.0 2.3 copy-start.19
  (3 other events, 2.2 us)
Sparse Core Ops, SparseCore 0:
  9.6 44.1 all-gather.5
  55.4 42.6 all-gather.9
  99.6 42.3 all-gather.7
  156.3 40.2 reduce-scatter.4
  198.8 40.6 reduce-scatter.2
  288.1 32.1 all-reduce.1
where the time goes:
time: 330 us; the launch traced here: 329 us
  waiting for transfers between devices  168 us (51%)
  blocking collectives  77.3 us (23%)
  matrix products  35.3 us (11%)
  starting transfers between devices  17.2 us (5%)
  between operations  14.8 us (4%)
  local copies, waits for them, and re-layouts  12.5 us (4%)
  other arithmetic  3.56 us (1%)
    all_gather x1, waiting for transfers between devices, local(): portion = lax.all_gather(expert_in, 'ctx', axis=0, tiled=True)  39.3 us
    reduce_scatter x1, waiting for transfers between devices, local(): lax.psum_scatter(jnp.dot(activated, w_down, preferred_element_type=f32).a...  34.4 us
    reduce_scatter x1, waiting for transfers between devices, local(): lax.psum_scatter((jnp.dot(grad_gate_pre, w_gate, preferred_element_type=f...  31.1 us
    all_gather x2, blocking collectives, carried_in(): gathered = lax.all_gather(value.astype(jnp.bfloat16), axis)  30.8 us
    all_gather x1, waiting for transfers between devices, local(): lax.all_gather(grad_in, 'ctx', axis=0, tiled=True)  28.6 us
    psum x1, waiting for transfers between devices, local(): lax.psum(state_part.astype(jnp.bfloat16), 'ctx').astype(jnp.float32)  27.7 us
    psum x1, blocking collectives, local(): inner_sum = lax.psum(jnp.sum(stream_f * scaled_grad, -1), 'ep')  14.5 us
    dot_general x4, matrix products, contract_last(): lax.dot_general(left, right, (((1,), (1,)), ((), ())), preferred_element_...  11.8 us
  transfers between devices with their start and end apart: 10, of which 6 were waited for; matrix products, arithmetic and copies ran while one was open for 10% of the time, Pallas kernels for 0%

commit v1 on v0

v1 whole, which is shorter than its diff:
```python
import functools

import jax
import jax.numpy as jnp
from jax import lax
from jax.experimental import pallas as pl
from jax.experimental.pallas import tpu as pltpu
from jax.sharding import PartitionSpec as P

MESH = pl.DeviceIdType.MESH


def exchange_kernel(axis, sources, places, *refs):
    count = len(sources)
    inputs, outputs = refs[:count], refs[count : 2 * count]
    send_sem, recv_sem, own_sem = refs[2 * count :]
    total = lax.axis_size(axis)
    me = lax.axis_index(axis)
    barrier = pltpu.get_barrier_semaphore()
    for step in range(1, total):
        pl.semaphore_signal(
            barrier, inc=1, device_id={axis: lax.rem(me + step, total)}, device_id_type=MESH
        )
    pl.semaphore_wait(barrier, total - 1)
    copies = []
    for step in range(1, total):
        peer = lax.rem(me + step, total)
        for item in range(count):
            copy = pltpu.make_async_remote_copy(
                src_ref=sources[item](inputs[item], peer),
                dst_ref=places[item](outputs[item], me),
                send_sem=send_sem.at[item, step - 1],
                recv_sem=recv_sem.at[item, step - 1],
                device_id={axis: peer},
                device_id_type=MESH,
            )
            copy.start()
            copies.append(copy)
    for item in range(count):
        own = pltpu.make_async_copy(
            sources[item](inputs[item], me), places[item](outputs[item], me), own_sem.at[item]
        )
        own.start()
        copies.append(own)
    for copy in copies:
        copy.wait()


def whole_ref(ref, peer):
    return ref


def leading(ref, place):
    return ref.at[place]


def second(ref, place):
    return ref.at[:, place]


def lanes(width):
    def pick(ref, place):
        start = pl.multiple_of(place * width, width)
        if len(ref.shape) == 2:
            return ref.at[:, pl.ds(start, width)]
        return ref.at[:, :, pl.ds(start, width)]

    return pick


def exchange(axis, ident, items):
    total = lax.axis_size(axis)
    count = len(items)
    result = pl.pallas_call(
        functools.partial(
            exchange_kernel, axis, [item[1] for item in items], [item[3] for item in items]
        ),
        out_shape=[jax.ShapeDtypeStruct(item[2], item[0].dtype) for item in items],
        in_specs=[pl.BlockSpec(memory_space=pl.ANY)] * count,
        out_specs=[pl.BlockSpec(memory_space=pl.ANY)] * count,
        scratch_shapes=[
            pltpu.SemaphoreType.DMA((count, total - 1)),
            pltpu.SemaphoreType.DMA((count, total - 1)),
            pltpu.SemaphoreType.DMA((count,)),
        ],
        compiler_params=pltpu.CompilerParams(collective_id=ident, has_side_effects=True),
        name=f"exchange_{ident}",
    )(*[item[0] for item in items])
    return result


def column_parts(value, parts):
    width = value.shape[-1] // parts
    if width % 128 == 0:
        return value, lanes(width)
    split = value.reshape(value.shape[:-1] + (parts, width))
    return jnp.moveaxis(split, -2, 0), leading


def spread_kernel(block_ref, all_ref, z_send, z_recv, xy_send, xy_recv, pair_send, pair_recv, own_sem):
    rows, width = block_ref.shape
    blocks = lax.axis_size("ctx")
    chips = lax.axis_size("ep") // 2
    my_block = lax.axis_index("ctx")
    my_ep = lax.axis_index("ep")
    chip = my_ep // 2
    core = lax.rem(my_ep, 2)

    def at(block, place):
        row = pl.multiple_of(block * rows, rows)
        column = pl.multiple_of(place * width, width)
        return all_ref.at[pl.ds(row, rows), pl.ds(column, width)]

    barrier = pltpu.get_barrier_semaphore()
    for step in range(1, blocks):
        pl.semaphore_signal(
            barrier, inc=1, device_id={"ctx": lax.rem(my_block + step, blocks)}, device_id_type=MESH
        )
    for step in range(1, chips):
        pl.semaphore_signal(
            barrier,
            inc=1,
            device_id={"ep": 2 * lax.rem(chip + step, chips) + core},
            device_id_type=MESH,
        )
    pl.semaphore_signal(
        barrier, inc=1, device_id={"ep": 2 * chip + 1 - core}, device_id_type=MESH
    )
    pl.semaphore_wait(barrier, blocks + chips - 1)
    z_copies = []
    for step in range(1, blocks):
        copy = pltpu.make_async_remote_copy(
            src_ref=block_ref,
            dst_ref=at(my_block, my_ep),
            send_sem=z_send.at[step - 1],
            recv_sem=z_recv.at[step - 1],
            device_id={"ctx": lax.rem(my_block + step, blocks)},
            device_id_type=MESH,
        )
        copy.start()
        z_copies.append(copy)
    own = pltpu.make_async_copy(block_ref, at(my_block, my_ep), own_sem)
    own.start()
    xy_copies = {}
    pair_copies = []

    def to_pair(back, turn):
        block = lax.rem(my_block - back + blocks, blocks)
        place = 2 * lax.rem(chip - turn + chips, chips) + core
        source = block_ref if back == 0 and turn == 0 else at(block, place)
        copy = pltpu.make_async_remote_copy(
            src_ref=source,
            dst_ref=at(block, place),
            send_sem=pair_send.at[back * chips + turn],
            recv_sem=pair_recv.at[back * chips + turn],
            device_id={"ep": 2 * chip + 1 - core},
            device_id_type=MESH,
        )
        copy.start()
        pair_copies.append(copy)

    for back in range(blocks + 1):
        if back < blocks:
            block = lax.rem(my_block - back + blocks, blocks)
            if back > 0:
                z_copies[back - 1].wait_recv()
            for step in range(1, chips):
                slot = back * (chips - 1) + step - 1
                copy = pltpu.make_async_remote_copy(
                    src_ref=block_ref if back == 0 else at(block, my_ep),
                    dst_ref=at(block, my_ep),
                    send_sem=xy_send.at[slot],
                    recv_sem=xy_recv.at[slot],
                    device_id={"ep": 2 * lax.rem(chip + step, chips) + core},
                    device_id_type=MESH,
                )
                copy.start()
                xy_copies[back, step] = copy
            to_pair(back, 0)
        if back > 0:
            for step in range(1, chips):
                xy_copies[back - 1, step].wait_recv()
                to_pair(back - 1, step)
    own.wait()
    for copy in z_copies + list(xy_copies.values()):
        copy.wait_send()
    for copy in pair_copies:
        copy.wait()


def spread(block, ident):
    blocks = lax.axis_size("ctx")
    parts = lax.axis_size("ep")
    rows, width = block.shape
    if blocks * parts > 64 or width % 128:
        return lax.all_gather(
            lax.all_gather(block, "ep", axis=1, tiled=True), "ctx", axis=0, tiled=True
        )
    chips = parts // 2
    dma = pltpu.SemaphoreType.DMA
    return pl.pallas_call(
        spread_kernel,
        out_shape=jax.ShapeDtypeStruct((blocks * rows, parts * width), block.dtype),
        in_specs=[pl.BlockSpec(memory_space=pl.ANY)],
        out_specs=pl.BlockSpec(memory_space=pl.ANY),
        scratch_shapes=[
            dma((blocks - 1,)),
            dma((blocks - 1,)),
            dma((blocks * (chips - 1),)),
            dma((blocks * (chips - 1),)),
            dma((blocks * chips,)),
            dma((blocks * chips,)),
            dma,
        ],
        compiler_params=pltpu.CompilerParams(collective_id=ident, has_side_effects=True),
        name=f"spread_{ident}",
    )(block)

def head_normalize(attended, gain):
    factor = lax.rsqrt(jnp.mean(attended * attended, -1, keepdims=True) + 1e-06)
    return attended * factor * gain


def contract_last(left, right):
    return lax.dot_general(
        left, right, (((1,), (1,)), ((), ())), preferred_element_type=jnp.float32
    )


def local(
    query_act,
    key_act,
    value_act,
    state_init,
    head_gain,
    out_weight,
    stream_in,
    model_gain,
    expert_ids,
    expert_slots,
    route_gates,
    gate_weight,
    up_weight,
    down_weight,
    out_grad,
):
    f32 = jnp.float32
    bf16 = jnp.bfloat16
    high = lax.Precision.HIGHEST
    ep_count = lax.axis_size("ep")
    ctx_count = lax.axis_size("ctx")
    expert_count = ep_count // 2
    my_ep = lax.axis_index("ep")
    my_ctx = lax.axis_index("ctx")
    tokens_here = query_act.shape[0]
    head_count = state_init.shape[0]
    head_size = state_init.shape[1]
    heads_width = head_count * head_size
    model_width = model_gain.shape[0]
    columns = stream_in.shape[1]
    capacity = 5 * tokens_here // (2 * expert_count)
    slots_all = ctx_count * capacity
    w_cols = lax.all_gather(out_weight, "ctx", axis=0, tiled=True)
    grads_all = lax.all_gather(
        lax.all_gather(out_grad, "ctx", axis=0, tiled=True), "ep", axis=1, tiled=True
    )
    query3 = query_act.reshape(tokens_here, head_count, head_size)
    key3 = key_act.reshape(tokens_here, head_count, head_size)
    value3 = value_act.reshape(tokens_here, head_count, head_size)
    kv_own = jnp.einsum("thd,the->hde", key3, value3, preferred_element_type=f32)
    meta = jnp.concatenate(
        [expert_ids.T.astype(f32), expert_slots.T.astype(f32), route_gates.T, route_gates.T], 0
    )
    kv_all, meta_all = exchange(
        "ctx",
        1,
        [
            (kv_own.astype(bf16), whole_ref, (ctx_count,) + kv_own.shape, leading),
            (meta, whole_ref, (ctx_count,) + meta.shape, leading),
        ],
    )
    earlier = (jnp.arange(ctx_count) < my_ctx).astype(f32)
    prefix = state_init + jnp.sum(earlier[:, None, None, None] * kv_all.astype(f32), 0)
    causal = jnp.arange(tokens_here)[:, None] >= jnp.arange(tokens_here)[None, :]
    scores = jnp.einsum("thd,shd->hts", query3, key3, preferred_element_type=f32)
    scores_bf = jnp.where(causal[None], scores, 0.0).astype(bf16)
    inside = jnp.einsum("hts,she->the", scores_bf, value3, preferred_element_type=f32)
    from_state = jnp.einsum("thd,hde->the", query3.astype(f32), prefix, precision=high)
    attended = from_state + inside
    gain_heads = head_gain.reshape(head_count, head_size)
    normed_heads = (
        head_normalize(attended, gain_heads).astype(bf16).reshape(tokens_here, heads_width)
    )
    normed_all = exchange(
        "ep",
        2,
        [(normed_heads, whole_ref, (tokens_here, ep_count * heads_width), lanes(heads_width))],
    )[0]
    attn_proj = jnp.dot(normed_all, w_cols, preferred_element_type=f32)
    stream = (stream_in.astype(f32) + attn_proj).astype(bf16)
    stream_f = stream.astype(f32)
    gain_cols = lax.dynamic_slice_in_dim(model_gain, my_ep * columns, columns, 0)
    all_rows = spread(stream, 3).astype(f32)
    scale_all = lax.rsqrt(jnp.mean(all_rows * all_rows, -1, keepdims=True) + 1e-05)
    model_in = (all_rows * scale_all * model_gain).astype(bf16)
    row_scale = lax.dynamic_slice_in_dim(scale_all, my_ctx * tokens_here, tokens_here, 0)
    ids_all = meta_all[:, 0:2]
    slots_of = meta_all[:, 2:4]
    gates_all = meta_all[:, 4:6]
    slot_iota = jnp.arange(capacity).astype(f32)
    my_expert = lax.rem(my_ep, expert_count).astype(f32)
    own_hits = (ids_all[:, :, None, :] == my_expert) & (
        slots_of[:, :, None, :] == slot_iota[None, None, :, None]
    )
    own_select = jnp.sum(own_hits.astype(f32), 1).astype(bf16)
    slot_gates = jnp.sum(jnp.where(own_hits, gates_all[:, :, None, :], 0.0), (1, 3))

    def pick_rows(rows):
        return jnp.einsum(
            "cst,ctd->csd",
            own_select,
            rows.reshape(ctx_count, tokens_here, model_width),
            preferred_element_type=f32,
        )

    grad_rows = (
        (pick_rows(grads_all) * slot_gates[:, :, None])
        .astype(bf16)
        .reshape(slots_all, model_width)
    )
    w_gate = gate_weight[0]
    w_up = up_weight[0]
    w_down = down_weight[0]
    portion = pick_rows(model_in).astype(bf16).reshape(slots_all, model_width)
    pre_gate = contract_last(portion, w_gate)
    pre_up = contract_last(portion, w_up)
    gate_sig = jax.nn.sigmoid(pre_gate)
    activated = (pre_gate * gate_sig * pre_up).astype(bf16)
    half_out = lax.psum_scatter(
        jnp.dot(activated, w_down, preferred_element_type=f32).astype(bf16),
        "ctx",
        scatter_dimension=0,
        tiled=True,
    )
    grad_act = contract_last(grad_rows, w_down)
    grad_gate_pre = (grad_act * pre_up * gate_sig * (1.0 + pre_gate * (1.0 - gate_sig))).astype(
        bf16
    )
    grad_up_pre = (grad_act * pre_gate * gate_sig).astype(bf16)
    grad_half = (
        jnp.dot(grad_gate_pre, w_gate, preferred_element_type=f32)
        + jnp.dot(grad_up_pre, w_up, preferred_element_type=f32)
    ).astype(bf16)
    grad_parts, part_of = column_parts(
        grad_half.reshape(ctx_count, capacity, model_width), ep_count
    )
    grad_back = exchange(
        "ep", 4, [(grad_parts, part_of, (ctx_count, ep_count, capacity, columns), second)]
    )[0]
    expert_of = (jnp.arange(ep_count) % expert_count).astype(f32)
    hits = (ids_all[:, :, :, None, None] == expert_of[None, None, None, :, None]) & (
        slots_of[:, :, :, None, None] == slot_iota[None, None, None, None, :]
    )
    picks = jnp.sum(hits.astype(f32), 1).astype(bf16)
    grad_tokens = jnp.einsum(
        "ctr,crd->ctd",
        picks.reshape(ctx_count, tokens_here, ep_count * capacity),
        grad_back.reshape(ctx_count, ep_count * capacity, columns),
        preferred_element_type=f32,
    ).astype(bf16)
    grad_terms = exchange("ctx", 5, [(grad_tokens, leading, grad_tokens.shape, leading)])[0]
    grad_model_in = jnp.sum(grad_terms.astype(f32), 0)
    scaled_grad = grad_model_in * gain_cols
    inner_own = jnp.sum(stream_f * scaled_grad, -1)
    inner_terms = exchange(
        "ep",
        6,
        [
            (
                jnp.broadcast_to(inner_own[None], (8, tokens_here)),
                whole_ref,
                (ep_count, 8, tokens_here),
                leading,
            )
        ],
    )[0]
    inner_sum = jnp.sum(inner_terms[:, 0], 0)
    grad_out = out_grad.astype(f32)
    grad_stream = (
        grad_out
        + row_scale * scaled_grad
        - stream_f * row_scale**3 * inner_sum[:, None] / model_width
    ).astype(bf16)
    head_parts = contract_last(grad_stream, w_cols).astype(bf16)
    out_parts, out_of = column_parts(half_out, ep_count)
    head_terms, returned = exchange(
        "ep",
        7,
        [
            (head_parts, lanes(heads_width), (ep_count, tokens_here, heads_width), leading),
            (out_parts, out_of, (ep_count, capacity, columns), leading),
        ],
    )
    grad_heads = jnp.sum(head_terms.astype(f32), 0)
    local_hits = (expert_ids[:, :, None, None] == (jnp.arange(ep_count) % expert_count)[:, None]) & (
        expert_slots[:, :, None, None] == jnp.arange(capacity)
    )
    dest_weights = jnp.sum(
        local_hits.astype(f32) * route_gates[:, :, None, None], 1
    ).reshape(tokens_here, ep_count * capacity)
    expert_mix = jnp.dot(
        dest_weights, returned.reshape(ep_count * capacity, columns).astype(f32), precision=high
    )
    layer_out = (stream_f + expert_mix).astype(bf16)
    head_pull = jax.vjp(lambda value: head_normalize(value, gain_heads), attended)[1]
    grad_attended = head_pull(grad_heads.reshape(tokens_here, head_count, head_size))[0].astype(
        bf16
    )
    state_part = jnp.einsum("thd,the->hde", query3, grad_attended, preferred_element_type=f32)
    state_all = exchange(
        "ctx", 8, [(state_part.astype(bf16), whole_ref, (ctx_count,) + state_part.shape, leading)]
    )[0].astype(f32)
    after = (jnp.arange(ctx_count) > my_ctx).astype(f32)
    later_sum = jnp.sum(after[:, None, None, None] * state_all, 0)
    state_total = jnp.sum(state_all, 0)
    grad_scores = jnp.einsum("the,she->hts", grad_attended, value3, preferred_element_type=f32)
    grad_masked = jnp.where(causal[None], grad_scores, 0.0).astype(jnp.bfloat16)
    grad_att_f = grad_attended.astype(f32)
    grad_query = jnp.einsum("the,hde->thd", grad_att_f, prefix, precision=high) + jnp.einsum(
        "hts,shd->thd", grad_masked, key3, preferred_element_type=f32
    )
    grad_key = jnp.einsum(
        "the,hde->thd", value3.astype(f32), later_sum, precision=high
    ) + jnp.einsum("hts,thd->shd", grad_masked, query3, preferred_element_type=f32)
    grad_value = jnp.einsum(
        "thd,hde->the", key3.astype(f32), later_sum, precision=high
    ) + jnp.einsum("hts,the->she", scores_bf, grad_attended, preferred_element_type=f32)
    flat_shape = (tokens_here, head_count * head_size)
    return (
        layer_out,
        grad_query.astype(jnp.bfloat16).reshape(flat_shape),
        grad_key.astype(jnp.bfloat16).reshape(flat_shape),
        grad_value.astype(jnp.bfloat16).reshape(flat_shape),
        state_total,
        grad_stream,
    )


def solution(mesh):
    return jax.shard_map(
        local,
        mesh=mesh,
        in_specs=(
            P("ctx", "ep"),
            P("ctx", "ep"),
            P("ctx", "ep"),
            P("ep", None, None),
            P("ep"),
            P("ctx", "ep"),
            P("ctx", "ep"),
            P(),
            P("ctx", None),
            P("ctx", None),
            P("ctx", None),
            P("ep", "ctx", None),
            P("ep", "ctx", None),
            P("ep", "ctx", None),
            P("ctx", "ep"),
        ),
        out_specs=(
            P("ctx", "ep"),
            P("ctx", "ep"),
            P("ctx", "ep"),
            P("ctx", "ep"),
            P("ep", None, None),
            P("ctx", "ep"),
        ),
        check_vma=False,
    )
```

time: 330 us -> 214 us (0.65)
  waiting for transfers between devices: 168 us -> 0.74 us
  Pallas kernels: 0 us -> 123 us
  blocking collectives: 77.3 us -> 19.6 us
  starting transfers between devices: 17.2 us -> 0.12 us
  other arithmetic: 3.56 us -> 15.2 us
  local copies, waits for them, and re-layouts: 12.5 us -> 7.88 us
    pallas_call x0 -> x8, Pallas kernels: none -> 123 us  [the longest x7 84.1 us: exchange(): pl.pallas_call(functools.partial(exchange_kernel, axis, [item[1] for item...]
    all_gather x2 -> x1, waiting for transfers between devices: 68 us -> 0.01 us  [local(): lax.all_gather(lax.all_gather(out_grad, 'ctx', axis=0, tiled=True), 'ep',...]
    all_gather x5 -> x1, blocking collectives: 62.9 us -> 19.6 us  [local(): lax.all_gather(out_grad, 'ctx', axis=0, tiled=True)]
    reduce_scatter x1, waiting for transfers between devices: 34.4 us -> 0.01 us  [local(): lax.psum_scatter(jnp.dot(activated, w_down, preferred_element_type=f32).a...]
    reduce_scatter x1 -> x0, waiting for transfers between devices: 31.1 us -> none  [local(): lax.psum_scatter((jnp.dot(grad_gate_pre, w_gate, preferred_element_type=f...]
    psum x1 -> x0, waiting for transfers between devices: 27.7 us -> none  [local(): lax.psum(state_part.astype(jnp.bfloat16), 'ctx').astype(jnp.float32)]
    all_to_all x4 -> x0, starting transfers between devices: 16.8 us -> none  [the longest x1 5.17 us: local(): lax.all_to_all(grad_send, 'ep', split_axis=0, concat_axis=1, tiled=True)]
    psum x1 -> x0, blocking collectives: 14.5 us -> none  [local(): inner_sum = lax.psum(jnp.sum(stream_f * scaled_grad, -1), 'ep')]
  transfers between devices with their start and end apart: 10 -> 3, of which waited for: 6 -> 0; matrix products, arithmetic and copies ran while one was open for 10% -> 21% of each run, Pallas kernels for 0% -> 47%
where the time goes in v1:
time: 214 us; the launch traced here: 213 us
  Pallas kernels  123 us (57%)
  matrix products  32.4 us (15%)
  blocking collectives  19.6 us (9%)
  other arithmetic  15.2 us (7%)
  between operations  14.4 us (7%)
  local copies, waits for them, and re-layouts  7.88 us (4%)
    pallas_call x7, Pallas kernels, exchange(): pl.pallas_call(functools.partial(exchange_kernel, axis, [item[1] for item...  84.1 us
    pallas_call x1, Pallas kernels, spread(): pl.pallas_call(spread_kernel, out_shape=jax.ShapeDtypeStruct((blocks * ro...  38.5 us
    all_gather x1, blocking collectives, local(): lax.all_gather(out_grad, 'ctx', axis=0, tiled=True)  19.6 us
    dot_general x4, matrix products, contract_last(): lax.dot_general(left, right, (((1,), (1,)), ((), ())), preferred_element_...  9.45 us
  transfers between devices with their start and end apart: 3, of which 0 were waited for; matrix products, arithmetic and copies ran while one was open for 21% of the time, Pallas kernels for 47%

profile of v1, /device:TPU:0, one launch (start us, length us, event | category | flops | bytes accessed | tf_op | source)
XLA Modules:
  0.0 212.9 jit_solution(13068049652019314610)
XLA Ops:
  7.3 0.7 all-gather.3.cloned.1.call-update
  8.0 19.6 %all_gather.10 = bf16[512,384]{1,0:T(8,128)(2,1)} all-gather(bf16[128,384]{1,0:T(8,128)(2,1)} %param.29), channel_id=1, replica_groups=mesh['ctx'=4,'ep'=8] {'ctx'}, dimensions={0}, use_global_device_ids=true | all-gather | bytes 491520 | tf_op jit(solution)/shard_map/all_gather | solution.py:265
  27.7 1.0 copy.153
  28.7 1.0 copy.126
  29.6 0.7 convert_bitcast_fusion
  30.4 0.8 convolution_convert_fusion.4.refs_0_
  31.1 1.4 pad_maximum_fusion.refs_1_
  32.5 11.9 %exchange_1.1 = (bf16[4,2,128,128]{3,2,1,0:T(8,128)(2,1)}, f32[4,8,128]{2,1,0:T(8,128)}) custom-call(bf16[2,128,128]{2,1,0:T(8,128)(2,1)} %convolution_convert_fusion.4.refs_0_, f32[8,128]{1,0:T(8,128)} %pad_maximum_fusion.refs_1_), custom_call_target="tpu_custom_call" | custom-call | tf_op jit(solution)/shard_map/exchange_1/pallas_call | solution.py:74
  44.4 1.1 multiply_reduce_fusion
  45.4 0.9 add.87
  46.4 0.3 convolution_bitcast_fusion.6
  46.7 1.1 fusion.31
  48.1 0.7 copy.125.refs_0_
  48.8 9.2 %exchange_2.1 = bf16[128,2048]{1,0:T(8,128)(2,1)} custom-call(bf16[128,256]{1,0:T(8,128)(2,1)} %copy.125.refs_0_), custom_call_target="tpu_custom_call" | custom-call | tf_op jit(solution)/shard_map/exchange_2/pallas_call | solution.py:74
  58.0 0.7 broadcast_compare_fusion.3
  58.8 0.8 fusion.68
  60.1 2.7 %fusion.27.block_ref = bf16[128,384]{1,0:T(8,128)(2,1)} fusion(bf16[128,2048]{1,0:T(8,128)(2,1)} %exchange_2.1, bf16[2048,384]{1,0:T(8,128)(2,1)} %all-gather.3.cloned.1.call-done, bf16[128,384]{1,0:T(8,128)(2,1)S(1)} %copy-done.8), kind=kOutput, calls=%fused_computation.30 | convolution fusion | flops 201474048 | bytes 2293760 | tf_op jit(solution)/shard_map/dot_general | solution.py:299
  62.7 38.5 %spread_3.1 = bf16[512,3072]{1,0:T(8,128)(2,1)} custom-call(bf16[128,384]{1,0:T(8,128)(2,1)} %fusion.27.block_ref), custom_call_target="tpu_custom_call" | custom-call | tf_op jit(solution)/shard_map/spread_3/pallas_call | solution.py:201
  101.2 2.7 %fusion = f32[512]{0:T(512)S(1)} fusion(bf16[512,3072]{1,0:T(8,128)(2,1)} %spread_3.1), kind=kLoop, calls=%fused_computation.2 | loop fusion | flops 4718080 | bytes 3147776 | tf_op jit(solution)/shard_map/reduce_sum | solution.py:304
  104.1 1.2 fusion.2
  105.3 0.7 convolution_convert_fusion
  106.2 1.7 fusion.5
  108.0 1.7 fusion.9
  109.8 1.0 copy-done.14
  110.7 3.1 %fusion.22 = bf16[320,3072]{1,0:T(8,128)(2,1)} fusion(bf16[1,768,3072]{2,1,0:T(8,128)(2,1)S(1)} %bitcast.171, f32[320,768]{1,0:T(8,128)S(1)} %fusion.9, f32[320,768]{1,0:T(8,128)S(1)} %fusion.5), kind=kOutput, calls=%fused_computation.21 | convolution fusion | flops 1512407040 | bytes 8650752 | tf_op jit(solution)/shard_map/dot_general | solution.py:340
  114.2 0.3 convert_reduce_fusion
  114.6 2.7 %fusion.21 = bf16[4,80,3072]{2,1,0:T(8,128)(2,1)S(1)} fusion(bf16[4,128,3072]{2,1,0:T(8,128)(2,1)} %bitcast.149, f32[4,80]{1,0:T(4,128)S(1)} %get-tuple-element.40, bf16[4,80,128]{2,1,0:T(8,128)(2,1)S(1)} %get-tuple-element.41), kind=kOutput, calls=%fused_computation.20 | convolution fusion | flops 253624320 | bytes 5195008 | tf_op jit(solution)/shard_map/cst,ctd->csd/dot_general | solution.py:319
  117.3 4.6 %fusion.13 = f32[320,768]{1,0:T(8,128)S(1)} fusion(bf16[320,3072]{1,0:T(8,128)(2,1)S(1)} %bitcast.151, bf16[1,768,3072]{2,1,0:T(8,128)(2,1)} %param.28), kind=kOutput, calls=%fused_computation.15 | convolution fusion | flops 1509949440 | bytes 7667712 | tf_op jit(solution)/shard_map/dot_general | solution.py:225
  121.9 2.0 fusion.3
  124.0 3.1 %fusion.18 = bf16[320,3072]{1,0:T(8,128)(2,1)} fusion(f32[320,3072]{1,0:T(8,128)S(1)} %fusion.3, bf16[1,768,3072]{2,1,0:T(8,128)(2,1)S(1)} %bitcast.179, f32[320,768]{1,0:T(8,128)S(1)} %fusion.13, f32[320,768]{1,0:T(8,128)S(1)} %fusion.5), kind=kOutput, calls=%fused_computation.19 | convolution fusion | flops 1513390080 | bytes 12582912 | tf_op jit(solution)/shard_map/dot_general | solution.py:352
  127.0 24.4 %exchange_4.1 = bf16[4,8,80,384]{3,2,1,0:T(8,128)(2,1)} custom-call(bf16[4,80,3072]{2,1,0:T(8,128)(2,1)} %bitcast.152), custom_call_target="tpu_custom_call" | custom-call | tf_op jit(solution)/shard_map/exchange_4/pallas_call | solution.py:74
  151.5 3.0 %convolution_convert_fusion.2.refs_0_ = bf16[4,128,384]{2,1,0:T(8,128)(2,1)} fusion(bf16[4,128,640]{1,2,0:T(8,128)(2,1)S(1)} %bitcast.150, bf16[4,640,384]{2,1,0:T(8,128)(2,1)} %bitcast.148), kind=kOutput, calls=%fused_computation.25 | convolution fusion | flops 251854848 | bytes 3014656 | tf_op jit(solution)/shard_map/ctr,crd->ctd/dot_general | solution.py:365
  154.5 11.0 %exchange_5.1 = bf16[4,128,384]{2,1,0:T(8,128)(2,1)} custom-call(bf16[4,128,384]{2,1,0:T(8,128)(2,1)} %convolution_convert_fusion.2.refs_0_), custom_call_target="tpu_custom_call" | custom-call | tf_op jit(solution)/shard_map/exchange_5/pallas_call | solution.py:74
  165.5 1.1 convert_reduce_fusion.2
  166.7 0.6 broadcast_in_dim.38.refs_0_
  167.3 5.0 %exchange_6.1 = f32[8,8,128]{2,1,0:T(8,128)} custom-call(f32[8,128]{1,0:T(8,128)} %broadcast_in_dim.38.refs_0_), custom_call_target="tpu_custom_call" | custom-call | tf_op jit(solution)/shard_map/exchange_6/pallas_call | solution.py:74
  172.3 0.8 slice_reduce_fusion
  173.3 1.4 convolution_convert_fusion.1.refs_0_
  174.7 13.6 %exchange_7.1 = (bf16[8,128,256]{2,1,0:T(8,128)(2,1)}, bf16[8,80,384]{2,1,0:T(8,128)(2,1)}) custom-call(bf16[128,2048]{1,0:T(8,128)(2,1)} %convolution_convert_fusion.1.refs_0_, bf16[80,3072]{1,0:T(8,128)(2,1)} %reduce-scatter.2.cloned.1.call-done.refs_1_), custom_call_target="tpu_custom_call" | custom-call | tf_op jit(solution)/shard_map/exchange_7/pallas_call | solution.py:74
  188.3 1.2 convert_reduce_fusion.1
  189.8 0.8 fusion.36.refs_0_
  190.6 9.2 %exchange_8.1 = bf16[4,2,128,128]{3,2,1,0:T(8,128)(2,1)} custom-call(bf16[2,128,128]{2,1,0:T(8,128)(2,1)} %fusion.36.refs_0_), custom_call_target="tpu_custom_call" | custom-call | tf_op jit(solution)/shard_map/exchange_8/pallas_call | solution.py:74
  199.8 1.7 convert_reduce_fusion.3
  201.5 0.3 fusion.47
  202.7 0.7 copy.118
  203.6 0.7 copy.117
  204.5 0.7 copy.116
  205.2 1.2 fusion.26
  (93 shorter events, 3.5 us)
Async XLA Ops:
  7.2 23.2 %copy-start = (bf16[128,256]{1,0:T(8,128)(2,1)S(1)}, bf16[128,256]{1,0:T(8,128)(2,1)}, u32[]{:S(2)}) copy-start(bf16[128,256]{1,0:T(8,128)(2,1)} %param.17) | copy-start | bytes 196612
  7.2 52.7 %copy-start.12 = (s32[128,2]{0,1:T(2,128)S(1)}, s32[128,2]{0,1:T(2,128)}, u32[]{:S(2)}) copy-start(s32[128,2]{0,1:T(2,128)} %param.23) | copy-start | bytes 3076
  7.2 52.8 %copy-start.13 = (s32[128,2]{0,1:T(2,128)S(1)}, s32[128,2]{0,1:T(2,128)}, u32[]{:S(2)}) copy-start(s32[128,2]{0,1:T(2,128)} %param.24) | copy-start | bytes 3076
  7.2 40.8 %copy-start.10 = (f32[256]{0:T(256)S(1)}, f32[256]{0:T(256)}, u32[]{:S(2)}) copy-start(f32[256]{0:T(256)} %param.19) | copy-start | bytes 3076
  7.2 52.8 %copy-start.8 = (bf16[128,384]{1,0:T(8,128)(2,1)S(1)}, bf16[128,384]{1,0:T(8,128)(2,1)}, u32[]{:S(2)}) copy-start(bf16[128,384]{1,0:T(8,128)(2,1)} %param.21) | copy-start | bytes 294916
  7.2 52.8 %all-gather.3.cloned.1.call-start = ((), (), s32[]{:S(2)}) async-start(), calls=%async_computation.1 | async-start | bytes 1966080 | tf_op jit(solution)/shard_map/all_gather | solution.py:263
  8.0 106.6 %all-gather.5.cloned.1.call-start = ((), (), s32[]{:S(2)}) async-start(), calls=%async_computation.2 | async-start | bytes 3538944 | tf_op jit(solution)/shard_map/all_gather | solution.py:264
  27.6 147.0 %reduce-scatter.2.cloned.1.call-start = ((), (), s32[]{:S(2)}) async-start(), calls=%async_computation.3 | async-start | bytes 2457600 | tf_op jit(solution)/shard_map/reduce_scatter | solution.py:339
  62.7 41.3 %copy-start.9 = (f32[3072]{0:T(1024)S(1)}, f32[3072]{0:T(1024)}, u32[]{:S(2)}) copy-start(f32[3072]{0:T(1024)} %param.22) | copy-start | bytes 36868
  101.2 2.8 %copy-start.1 = (bf16[512,3072]{1,0:T(8,128)(2,1)S(1)}, bf16[512,3072]{1,0:T(8,128)(2,1)}, u32[]{:S(2)}) copy-start(bf16[512,3072]{1,0:T(8,128)(2,1)} %spread_3.1) | copy-start | bytes 9437188
  104.0 2.2 %slice-start.2 = ((s8[4718592]{0:T(1024)(128)(4,1)}), s8[4194304]{0:T(1024)(128)(4,1)S(1)}, s32[]{:S(2)}) async-start(s8[4718592]{0:T(1024)(128)(4,1)} %bitcast.172), calls=%async_computation.6 | async-start | bytes 8388608
  104.1 2.1 %slice-start.3 = ((s8[4718592]{0:T(1024)(128)(4,1)}), s8[524288]{0:T(1024)(128)(4,1)S(1)}, s32[]{:S(2)}) async-start(s8[4718592]{0:T(1024)(128)(4,1)} %bitcast.172), calls=%async_computation.7 | async-start | bytes 1048576
  105.3 2.7 %slice-start.6 = ((s8[4718592]{0:T(1024)(128)(4,1)}), s8[4194304]{0:T(1024)(128)(4,1)S(1)}, s32[]{:S(2)}) async-start(s8[4718592]{0:T(1024)(128)(4,1)} %bitcast.176), calls=%async_computation.10 | async-start | bytes 8388608
  106.2 1.8 slice-start.7
  106.2 4.5 %slice-start = ((s8[4718592]{0:T(1024)(128)(4,1)}), s8[4194304]{0:T(1024)(128)(4,1)S(1)}, s32[]{:S(2)}) async-start(s8[4718592]{0:T(1024)(128)(4,1)} %bitcast.170), calls=%async_computation.4 | async-start | bytes 8388608
  108.0 2.8 %slice-start.1 = ((s8[4718592]{0:T(1024)(128)(4,1)}), s8[524288]{0:T(1024)(128)(4,1)S(1)}, s32[]{:S(2)}) async-start(s8[4718592]{0:T(1024)(128)(4,1)} %bitcast.170), calls=%async_computation.5 | async-start | bytes 1048576
  109.7 1.0 copy-start.14
  110.7 3.1 %copy-start.11 = (f32[128,2]{0,1:T(2,128)S(1)}, f32[128,2]{0,1:T(2,128)}, u32[]{:S(2)}) copy-start(f32[128,2]{0,1:T(2,128)} %param.25) | copy-start | bytes 3076
  114.6 7.3 %slice-start.4 = ((s8[4718592]{0:T(1024)(128)(4,1)}), s8[4194304]{0:T(1024)(128)(4,1)S(1)}, s32[]{:S(2)}) async-start(s8[4718592]{0:T(1024)(128)(4,1)} %bitcast.174), calls=%async_computation.8 | async-start | bytes 8388608
  117.3 4.6 %slice-start.5 = ((s8[4718592]{0:T(1024)(128)(4,1)}), s8[524288]{0:T(1024)(128)(4,1)S(1)}, s32[]{:S(2)}) async-start(s8[4718592]{0:T(1024)(128)(4,1)} %bitcast.174), calls=%async_computation.9 | async-start | bytes 1048576
  117.3 4.6 %copy-start.15 = (f32[320,768]{1,0:T(8,128)S(1)}, f32[320,768]{1,0:T(8,128)}, u32[]{:S(2)}) copy-start(f32[320,768]{1,0:T(8,128)} %copy-done.14) | copy-start | bytes 2949124
  117.3 6.7 %slice-start.8 = ((s8[4718592]{0:T(1024)(128)(4,1)}), s8[4194304]{0:T(1024)(128)(4,1)S(1)}, s32[]{:S(2)}) async-start(s8[4718592]{0:T(1024)(128)(4,1)} %bitcast.178), calls=%async_computation.12 | async-start | bytes 8388608
  121.9 2.0 slice-start.9
  151.4 15.1 %copy-start.3 = (bf16[128,384]{1,0:T(8,128)(2,1)S(1)}, bf16[128,384]{1,0:T(8,128)(2,1)}, u32[]{:S(2)}) copy-start(bf16[128,384]{1,0:T(8,128)(2,1)} %fusion.27.block_ref) | copy-start | bytes 294916
  151.5 21.6 %copy-start.6 = (bf16[128,384]{1,0:T(8,128)(2,1)S(1)}, bf16[128,384]{1,0:T(8,128)(2,1)}, u32[]{:S(2)}) copy-start(bf16[128,384]{1,0:T(8,128)(2,1)} %param.29) | copy-start | bytes 294916
  151.5 21.8 %copy-start.2 = (bf16[2048,384]{1,0:T(8,128)(2,1)S(1)}, bf16[2048,384]{1,0:T(8,128)(2,1)}, u32[]{:S(2)}) copy-start(bf16[2048,384]{1,0:T(8,128)(2,1)} %all-gather.3.cloned.1.call-done) | copy-start | bytes 4718596
  172.3 29.3 %copy-start.7 = (bf16[128,256]{1,0:T(8,128)(2,1)S(1)}, bf16[128,256]{1,0:T(8,128)(2,1)}, u32[]{:S(2)}) copy-start(bf16[128,256]{1,0:T(8,128)(2,1)} %param.16) | copy-start | bytes 196612
  173.3 28.8 %copy-start.5 = (bf16[128,384]{1,0:T(8,128)(2,1)}, bf16[128,384]{1,0:T(8,128)(2,1)S(1)}, u32[]{:S(2)}) copy-start(bf16[128,384]{1,0:T(8,128)(2,1)S(1)} %fusion.44) | copy-start | bytes 294916
  188.3 17.0 %copy-start.4 = (bf16[8,80,384]{2,1,0:T(8,128)(2,1)S(1)}, bf16[8,80,384]{2,1,0:T(8,128)(2,1)}, u32[]{:S(2)}) copy-start(bf16[8,80,384]{2,1,0:T(8,128)(2,1)} %get-tuple-element.12) | copy-start | bytes 1474564
Sparse Core Ops, SparseCore 0:
  9.6 46.8 all-gather.2
  58.3 43.1 all-gather.4
  114.0 40.4 reduce-scatter.1

commit v2 on v1

--- a/solution.py
+++ b/solution.py
@@ -10,22 +10,34 @@
 MESH = pl.DeviceIdType.MESH
 
 
-def exchange_kernel(axis, sources, places, *refs):
+def greet(axes):
+    barrier = pltpu.get_barrier_semaphore()
+    expected = 0
+    for axis in axes:
+        total = lax.axis_size(axis)
+        for step in range(1, total):
+            pl.semaphore_signal(
+                barrier,
+                inc=1,
+                device_id={axis: lax.rem(lax.axis_index(axis) + step, total)},
+                device_id_type=MESH,
+            )
+        expected += total - 1
+    pl.semaphore_wait(barrier, expected)
+
+
+def exchange_kernel(axes, sources, places, *refs):
     count = len(sources)
     inputs, outputs = refs[:count], refs[count : 2 * count]
     send_sem, recv_sem, own_sem = refs[2 * count :]
-    total = lax.axis_size(axis)
-    me = lax.axis_index(axis)
-    barrier = pltpu.get_barrier_semaphore()
-    for step in range(1, total):
-        pl.semaphore_signal(
-            barrier, inc=1, device_id={axis: lax.rem(me + step, total)}, device_id_type=MESH
-        )
-    pl.semaphore_wait(barrier, total - 1)
+    greet(sorted(set(axes)))
     copies = []
-    for step in range(1, total):
-        peer = lax.rem(me + step, total)
-        for item in range(count):
+    for item in range(count):
+        axis = axes[item]
+        total = lax.axis_size(axis)
+        me = lax.axis_index(axis)
+        for step in range(1, total):
+            peer = lax.rem(me + step, total)
             copy = pltpu.make_async_remote_copy(
                 src_ref=sources[item](inputs[item], peer),
                 dst_ref=places[item](outputs[item], me),
@@ -37,6 +49,7 @@
             copy.start()
             copies.append(copy)
     for item in range(count):
+        me = lax.axis_index(axes[item])
         own = pltpu.make_async_copy(
             sources[item](inputs[item], me), places[item](outputs[item], me), own_sem.at[item]
         )
@@ -69,11 +82,12 @@
 
 
 def exchange(axis, ident, items):
-    total = lax.axis_size(axis)
+    axes = [item[4] if len(item) > 4 else axis for item in items]
+    total = max(lax.axis_size(name) for name in axes)
     count = len(items)
     result = pl.pallas_call(
         functools.partial(
-            exchange_kernel, axis, [item[1] for item in items], [item[3] for item in items]
+            exchange_kernel, axes, [item[1] for item in items], [item[3] for item in items]
         ),
         out_shape=[jax.ShapeDtypeStruct(item[2], item[0].dtype) for item in items],
         in_specs=[pl.BlockSpec(memory_space=pl.ANY)] * count,
@@ -95,6 +109,140 @@
         return value, lanes(width)
     split = value.reshape(value.shape[:-1] + (parts, width))
     return jnp.moveaxis(split, -2, 0), leading
+
+
+def combine_kernel(
+    rows_ref, picks_ref, stream_ref, gain_ref, grad_ref, inner_ref,
+    landed, outgoing, arrived, inner_own, inner_all,
+    own_sem, send_sem, recv_sem, z_send, z_recv, i_send, i_recv,
+):
+    f32 = jnp.float32
+    blocks = lax.axis_size("ctx")
+    parts = lax.axis_size("ep")
+    experts = picks_ref.shape[1]
+    width = stream_ref.shape[1]
+    my_block = lax.axis_index("ctx")
+    my_ep = lax.axis_index("ep")
+    greet(["ctx", "ep"])
+
+    def block_at(step):
+        return lax.rem(my_block + step, blocks)
+
+    def columns_of(place):
+        return pl.ds(pl.multiple_of(place * width, width), width)
+
+    order = list(range(1, blocks)) + [0]
+    copies = {}
+    for step in order:
+        block = block_at(step)
+        for turn in range(1, parts):
+            peer = lax.rem(my_ep + turn, parts)
+            copy = pltpu.make_async_remote_copy(
+                src_ref=rows_ref.at[block, :, columns_of(peer)],
+                dst_ref=landed.at[block, my_ep],
+                send_sem=send_sem.at[step, turn - 1],
+                recv_sem=recv_sem.at[step, turn - 1],
+                device_id={"ep": peer},
+                device_id_type=MESH,
+            )
+            copy.start()
+            copies[step, turn] = copy
+    own = pltpu.make_async_copy(
+        rows_ref.at[:, :, columns_of(my_ep)], landed.at[:, my_ep], own_sem
+    )
+    own.start()
+    own.wait()
+    z_copies = []
+    total = None
+    for step in order:
+        block = block_at(step)
+        for turn in range(1, parts):
+            copies[step, turn].wait_recv()
+        total = jnp.dot(picks_ref[block, 0], landed[block, 0], preferred_element_type=f32)
+        for place in range(1, parts):
+            total += jnp.dot(
+                picks_ref[block, place % experts],
+                landed[block, place],
+                preferred_element_type=f32,
+            )
+        if step:
+            outgoing[step - 1] = total.astype(outgoing.dtype)
+            copy = pltpu.make_async_remote_copy(
+                src_ref=outgoing.at[step - 1],
+                dst_ref=arrived.at[step - 1],
+                send_sem=z_send.at[step - 1],
+                recv_sem=z_recv.at[step - 1],
+                device_id={"ctx": block},
+                device_id_type=MESH,
+            )
+            copy.start()
+            z_copies.append(copy)
+    for step in range(1, blocks):
+        z_copies[step - 1].wait_recv()
+        total += arrived[step - 1].astype(f32)
+    grad_ref[...] = total
+    weighed = stream_ref[...].astype(f32) * total * gain_ref[...]
+    inner_own[...] = lax.dot_general(
+        jnp.ones((8, width), f32),
+        weighed,
+        (((1,), (1,)), ((), ())),
+        precision=lax.Precision.HIGHEST,
+        preferred_element_type=f32,
+    )
+    i_copies = []
+    for turn in range(1, parts):
+        copy = pltpu.make_async_remote_copy(
+            src_ref=inner_own,
+            dst_ref=inner_all.at[turn - 1],
+            send_sem=i_send.at[turn - 1],
+            recv_sem=i_recv.at[turn - 1],
+            device_id={"ep": lax.rem(my_ep + turn, parts)},
+            device_id_type=MESH,
+        )
+        copy.start()
+        i_copies.append(copy)
+    inner = inner_own[...]
+    for turn in range(1, parts):
+        i_copies[turn - 1].wait_recv()
+        inner += inner_all[turn - 1]
+    inner_ref[...] = inner
+    for copy in list(copies.values()) + z_copies + i_copies:
+        copy.wait_send()
+
+
+def combine(rows, picks, stream, gain, ident):
+    blocks, capacity, _ = rows.shape
+    parts = lax.axis_size("ep")
+    tokens, width = stream.shape
+    dma = pltpu.SemaphoreType.DMA
+    vmem = pl.BlockSpec(memory_space=pltpu.VMEM)
+    return pl.pallas_call(
+        combine_kernel,
+        out_shape=[
+            jax.ShapeDtypeStruct((tokens, width), jnp.float32),
+            jax.ShapeDtypeStruct((8, tokens), jnp.float32),
+        ],
+        in_specs=[pl.BlockSpec(memory_space=pl.ANY), vmem, vmem, vmem],
+        out_specs=[vmem, vmem],
+        scratch_shapes=[
+            pltpu.VMEM((blocks, parts, capacity, width), jnp.bfloat16),
+            pltpu.VMEM((blocks - 1, tokens, width), jnp.bfloat16),
+            pltpu.VMEM((blocks - 1, tokens, width), jnp.bfloat16),
+            pltpu.VMEM((8, tokens), jnp.float32),
+            pltpu.VMEM((parts - 1, 8, tokens), jnp.float32),
+            dma,
+            dma((blocks, parts - 1)),
+            dma((blocks, parts - 1)),
+            dma((blocks - 1,)),
+            dma((blocks - 1,)),
+            dma((parts - 1,)),
+            dma((parts - 1,)),
+        ],
+        compiler_params=pltpu.CompilerParams(
+            collective_id=ident, has_side_effects=True, vmem_limit_bytes=24 * 1024 * 1024
+        ),
+        name=f"combine_{ident}",
+    )(rows, picks, stream, gain)
 
 
 def spread_kernel(block_ref, all_ref, z_send, z_recv, xy_send, xy_recv, pair_send, pair_recv, own_sem):
@@ -261,9 +409,6 @@
     capacity = 5 * tokens_here // (2 * expert_count)
     slots_all = ctx_count * capacity
     w_cols = lax.all_gather(out_weight, "ctx", axis=0, tiled=True)
-    grads_all = lax.all_gather(
-        lax.all_gather(out_grad, "ctx", axis=0, tiled=True), "ep", axis=1, tiled=True
-    )
     query3 = query_act.reshape(tokens_here, head_count, head_size)
     key3 = key_act.reshape(tokens_here, head_count, head_size)
     value3 = value_act.reshape(tokens_here, head_count, head_size)
@@ -271,13 +416,32 @@
     meta = jnp.concatenate(
         [expert_ids.T.astype(f32), expert_slots.T.astype(f32), route_gates.T, route_gates.T], 0
     )
-    kv_all, meta_all = exchange(
+    grad_item = (
+        (out_grad, whole_ref, (tokens_here, model_width), lanes(columns), "ep")
+        if columns % 128 == 0
+        else (out_grad, whole_ref, (ep_count, tokens_here, columns), leading, "ep")
+    )
+    kv_all, meta_all, grad_block = exchange(
         "ctx",
         1,
         [
             (kv_own.astype(bf16), whole_ref, (ctx_count,) + kv_own.shape, leading),
             (meta, whole_ref, (ctx_count,) + meta.shape, leading),
+            grad_item,
         ],
+    )
+    if grad_block.ndim == 3:
+        grad_block = jnp.moveaxis(grad_block, 0, 1).reshape(tokens_here, model_width)
+    here_hits = (expert_ids[:, :, None] == lax.rem(my_ep, expert_count)) & (
+        expert_slots[:, :, None] == jnp.arange(capacity)
+    )
+    here_select = jnp.sum(here_hits.astype(f32), 1).astype(bf16)
+    here_gates = jnp.sum(jnp.where(here_hits, route_gates[:, :, None], 0.0), (0, 1))
+    grad_own = lax.dot_general(
+        here_select, grad_block, (((0,), (0,)), ((), ())), preferred_element_type=f32
+    )
+    grad_rows = lax.all_gather(
+        (grad_own * here_gates[:, None]).astype(bf16), "ctx", axis=0, tiled=True
     )
     earlier = (jnp.arange(ctx_count) < my_ctx).astype(f32)
     prefix = state_init + jnp.sum(earlier[:, None, None, None] * kv_all.astype(f32), 0)
@@ -306,14 +470,12 @@
     row_scale = lax.dynamic_slice_in_dim(scale_all, my_ctx * tokens_here, tokens_here, 0)
     ids_all = meta_all[:, 0:2]
     slots_of = meta_all[:, 2:4]
-    gates_all = meta_all[:, 4:6]
     slot_iota = jnp.arange(capacity).astype(f32)
     my_expert = lax.rem(my_ep, expert_count).astype(f32)
     own_hits = (ids_all[:, :, None, :] == my_expert) & (
         slots_of[:, :, None, :] == slot_iota[None, None, :, None]
     )
     own_select = jnp.sum(own_hits.astype(f32), 1).astype(bf16)
-    slot_gates = jnp.sum(jnp.where(own_hits, gates_all[:, :, None, :], 0.0), (1, 3))
 
     def pick_rows(rows):
         return jnp.einsum(
@@ -323,11 +485,6 @@
             preferred_element_type=f32,
         )
 
-    grad_rows = (
-        (pick_rows(grads_all) * slot_gates[:, :, None])
-        .astype(bf16)
-        .reshape(slots_all, model_width)
-    )
     w_gate = gate_weight[0]
     w_up = up_weight[0]
     w_down = down_weight[0]
@@ -351,40 +508,41 @@
         jnp.dot(grad_gate_pre, w_gate, preferred_element_type=f32)
         + jnp.dot(grad_up_pre, w_up, preferred_element_type=f32)
     ).astype(bf16)
-    grad_parts, part_of = column_parts(
-        grad_half.reshape(ctx_count, capacity, model_width), ep_count
-    )
-    grad_back = exchange(
-        "ep", 4, [(grad_parts, part_of, (ctx_count, ep_count, capacity, columns), second)]
-    )[0]
-    expert_of = (jnp.arange(ep_count) % expert_count).astype(f32)
-    hits = (ids_all[:, :, :, None, None] == expert_of[None, None, None, :, None]) & (
-        slots_of[:, :, :, None, None] == slot_iota[None, None, None, None, :]
+    grad_half = grad_half.reshape(ctx_count, capacity, model_width)
+    expert_of = jnp.arange(expert_count).astype(f32)
+    hits = (ids_all[:, :, None, :, None] == expert_of[None, None, :, None, None]) & (
+        slots_of[:, :, None, :, None] == slot_iota[None, None, None, None, :]
     )
     picks = jnp.sum(hits.astype(f32), 1).astype(bf16)
-    grad_tokens = jnp.einsum(
-        "ctr,crd->ctd",
-        picks.reshape(ctx_count, tokens_here, ep_count * capacity),
-        grad_back.reshape(ctx_count, ep_count * capacity, columns),
-        preferred_element_type=f32,
-    ).astype(bf16)
-    grad_terms = exchange("ctx", 5, [(grad_tokens, leading, grad_tokens.shape, leading)])[0]
-    grad_model_in = jnp.sum(grad_terms.astype(f32), 0)
-    scaled_grad = grad_model_in * gain_cols
-    inner_own = jnp.sum(stream_f * scaled_grad, -1)
-    inner_terms = exchange(
-        "ep",
-        6,
-        [
-            (
-                jnp.broadcast_to(inner_own[None], (8, tokens_here)),
-                whole_ref,
-                (ep_count, 8, tokens_here),
-                leading,
-            )
-        ],
-    )[0]
-    inner_sum = jnp.sum(inner_terms[:, 0], 0)
+    if columns % 128 == 0 and ep_count * ctx_count <= 64:
+        grad_model_in, inner_rows = combine(grad_half, picks, stream, gain_cols[None], 4)
+        scaled_grad = grad_model_in * gain_cols
+        inner_sum = inner_rows[0]
+    else:
+        grad_parts, part_of = column_parts(grad_half, ep_count)
+        grad_back = exchange(
+            "ep", 4, [(grad_parts, part_of, (ctx_count, ep_count, capacity, columns), second)]
+        )[0].reshape(ctx_count, 2, expert_count, capacity, columns)
+        grad_tokens = jnp.einsum(
+            "cets,chesd->ctd", picks, grad_back, preferred_element_type=f32
+        ).astype(bf16)
+        grad_terms = exchange("ctx", 5, [(grad_tokens, leading, grad_tokens.shape, leading)])[0]
+        grad_model_in = jnp.sum(grad_terms.astype(f32), 0)
+        scaled_grad = grad_model_in * gain_cols
+        inner_own = jnp.sum(stream_f * scaled_grad, -1)
+        inner_terms = exchange(
+            "ep",
+            6,
+            [
+                (
+                    jnp.broadcast_to(inner_own[None], (8, tokens_here)),
+                    whole_ref,
+                    (ep_count, 8, tokens_here),
+                    leading,
+                )
+            ],
+        )[0]
+        inner_sum = jnp.sum(inner_terms[:, 0], 0)
     grad_out = out_grad.astype(f32)
     grad_stream = (
         grad_out

time: 214 us -> 188 us (0.88)
  blocking collectives: 19.6 us -> 0 us
  Pallas kernels: 123 us -> 109 us
  waiting for transfers between devices: 0.74 us -> 14.4 us
  matrix products: 32.4 us -> 29.8 us
    all_gather x1 -> x0, blocking collectives: 19.6 us -> none  [local(): lax.all_gather(out_grad, 'ctx', axis=0, tiled=True)]
    pallas_call x1, Pallas kernels: 38.5 us -> 22.7 us  [spread(): pl.pallas_call(spread_kernel, out_shape=jax.ShapeDtypeStruct((blocks * ro...]
    all_gather x1, waiting for transfers between devices: 0.01 us -> 8.33 us  [local(): lax.all_gather((grad_own * here_gates[:, None]).astype(bf16), 'ctx', axis...]
    all_gather x1, waiting for transfers between devices: 0.02 us -> 4.45 us  [local(): w_cols = lax.all_gather(out_weight, 'ctx', axis=0, tiled=True)]
    dot_general x2 -> x1, matrix products: 3.38 us -> 0.67 us  [pick_rows(): jnp.einsum('cst,ctd->csd', own_select, rows.reshape(ctx_count, tokens_her...]
    dot_general x1, matrix products: 2.01 us -> 4.63 us  [local(): jnp.dot(grad_gate_pre, w_gate, preferred_element_type=f32)]
    pallas_call x7 -> x5, Pallas kernels: 84.1 us -> 86.4 us  [the longest x4 51.5 us: exchange(): pl.pallas_call(functools.partial(exchange_kernel, axes, [item[1] for item...]
  transfers between devices with their start and end apart: 3 -> 3, of which waited for: 0 -> 3; matrix products, arithmetic and copies ran while one was open for 21% -> 21% of each run, Pallas kernels for 47% -> 45%
where the time goes in v2:
time: 188 us
  Pallas kernels  109 us (58%)
  matrix products  29.8 us (16%)
  waiting for transfers between devices  14.4 us (8%)
  between operations  14.4 us (8%)
  other arithmetic  13.7 us (7%)
  local copies, waits for them, and re-layouts  6.51 us (3%)
    pallas_call x4, Pallas kernels, exchange(): pl.pallas_call(functools.partial(exchange_kernel, axes, [item[1] for item...  51.5 us
    pallas_call x1, Pallas kernels, combine(): pl.pallas_call(combine_kernel, out_shape=[jax.ShapeDtypeStruct((tokens, w...  34.9 us
    pallas_call x1, Pallas kernels, spread(): pl.pallas_call(spread_kernel, out_shape=jax.ShapeDtypeStruct((blocks * ro...  22.7 us
    dot_general x4, matrix products, contract_last(): lax.dot_general(left, right, (((1,), (1,)), ((), ())), preferred_element_...  9.76 us
    all_gather x1, waiting for transfers between devices, local(): lax.all_gather((grad_own * here_gates[:, None]).astype(bf16), 'ctx', axis...  8.33 us
    dot_general x1, matrix products, local(): jnp.dot(grad_gate_pre, w_gate, preferred_element_type=f32)  4.63 us
    all_gather x1, waiting for transfers between devices, local(): w_cols = lax.all_gather(out_weight, 'ctx', axis=0, tiled=True)  4.45 us
  transfers between devices with their start and end apart: 3, of which 3 were waited for; matrix products, arithmetic and copies ran while one was open for 21% of the time, Pallas kernels for 45%

profile of v2, /device:TPU:0, one launch (start us, length us, event | category | flops | bytes accessed | tf_op | source)
XLA Modules:
  0.0 188.0 jit_solution(4747075715188501260)
XLA Ops:
  7.3 0.7 all-gather.3.cloned.1.call-update
  8.0 0.9 copy.153
  9.0 0.7 convert_bitcast_fusion
  9.7 1.4 pad_maximum_fusion.refs_1_
  11.0 0.8 convolution_convert_fusion.3.refs_0_
  11.8 18.1 %exchange_1.1 = (bf16[4,2,128,128]{3,2,1,0:T(8,128)(2,1)}, f32[4,8,128]{2,1,0:T(8,128)}, bf16[128,3072]{1,0:T(8,128)(2,1)}) custom-call(bf16[2,128,128]{2,1,0:T(8,128)(2,1)} %convolution_convert_fusion.3.refs_0_, f32[8,128]{1,0:T(8,128)} %pad_maximum_fusion.refs_1_, bf16[128,384]{1,0:T(8,128)(2,1)} %refs_2_.1), custom_call_target="tpu_custom_call" | custom-call | tf_op jit(solution)/shard_map/exchange_1/pallas_call | solution.py:88
  29.9 0.7 broadcast_compare_fusion.4
  30.6 0.8 convert_reduce_fusion.4
  31.4 2.2 %fusion.24 = bf16[80,3072]{1,0:T(8,128)(2,1)} fusion(bf16[128,3072]{1,0:T(8,128)(2,1)} %get-tuple-element.14, f32[80]{0:T(128)S(1)} %get-tuple-element.47, bf16[128,80]{0,1:T(8,128)(2,1)S(1)} %get-tuple-element.46), kind=kOutput, calls=%fused_computation.22 | convolution fusion | flops 63406080 | bytes 1298752 | tf_op jit(solution)/shard_map/dot_general | solution.py:440
  33.8 1.0 copy.126
  34.8 1.1 multiply_reduce_fusion
  35.9 0.9 add.79
  36.8 0.3 convolution_bitcast_fusion.6
  37.1 0.2 fusion.31
  37.3 0.2 multiply_reduce_fusion.2
  37.7 0.7 copy.125.refs_0_
  38.4 8.2 %exchange_2.1 = bf16[128,2048]{1,0:T(8,128)(2,1)} custom-call(bf16[128,256]{1,0:T(8,128)(2,1)} %copy.125.refs_0_), custom_call_target="tpu_custom_call" | custom-call | tf_op jit(solution)/shard_map/exchange_2/pallas_call | solution.py:88
  46.9 4.4 %all-gather.3.cloned.1.call-done = bf16[2048,384]{1,0:T(8,128)(2,1)} async-done(((bf16[512,384]{1,0:T(8,128)(2,1)}), bf16[2048,384]{1,0:T(8,128)(2,1)}) %all-gather.3.cloned.1.call-update) | async-done | bytes 1572880 | tf_op jit(solution)/shard_map/all_gather | solution.py:411
  51.4 2.7 %fusion.27.block_ref.stream_ref = bf16[128,384]{1,0:T(8,128)(2,1)} fusion(bf16[128,2048]{1,0:T(8,128)(2,1)} %exchange_2.1, bf16[2048,384]{1,0:T(8,128)(2,1)} %all-gather.3.cloned.1.call-done, bf16[128,384]{1,0:T(8,128)(2,1)S(1)} %copy-done.8), kind=kOutput, calls=%fused_computation.29 | convolution fusion | flops 201474048 | bytes 2293760 | tf_op jit(solution)/shard_map/dot_general | solution.py:463
  54.0 22.7 %spread_3.1 = bf16[512,3072]{1,0:T(8,128)(2,1)} custom-call(bf16[128,384]{1,0:T(8,128)(2,1)} %fusion.27.block_ref.stream_ref), custom_call_target="tpu_custom_call" | custom-call | tf_op jit(solution)/shard_map/spread_3/pallas_call | solution.py:349
  76.7 2.7 %fusion = f32[512]{0:T(512)S(1)} fusion(bf16[512,3072]{1,0:T(8,128)(2,1)} %spread_3.1), kind=kLoop, calls=%fused_computation.2 | loop fusion | flops 4718080 | bytes 3147776 | tf_op jit(solution)/shard_map/reduce_sum | solution.py:468
  79.6 1.2 fusion.2
  80.7 0.7 convolution_convert_fusion
  81.5 1.8 fusion.5
  83.3 1.8 fusion.9
  85.1 0.9 copy-done.15
  86.1 3.1 %fusion.21 = bf16[320,3072]{1,0:T(8,128)(2,1)} fusion(bf16[1,768,3072]{2,1,0:T(8,128)(2,1)S(1)} %bitcast.163, f32[320,768]{1,0:T(8,128)S(1)} %fusion.9, f32[320,768]{1,0:T(8,128)S(1)} %fusion.5), kind=kOutput, calls=%fused_computation.19 | convolution fusion | flops 1512407040 | bytes 8650752 | tf_op jit(solution)/shard_map/dot_general | solution.py:497
  89.6 0.3 copy.105.picks_ref
  90.2 8.3 %all-gather.5.cloned.1.call-done = bf16[320,3072]{1,0:T(8,128)(2,1)} async-done(((bf16[80,3072]{1,0:T(8,128)(2,1)}), bf16[320,3072]{1,0:T(8,128)(2,1)}) %all-gather.5.cloned.1.call-update) | async-done | bytes 1966096 | tf_op jit(solution)/shard_map/all_gather | solution.py:443
  98.5 4.8 %fusion.13 = f32[320,768]{1,0:T(8,128)S(1)} fusion(bf16[320,3072]{1,0:T(8,128)(2,1)} %all-gather.5.cloned.1.call-done, bf16[1,768,3072]{2,1,0:T(8,128)(2,1)} %param.28), kind=kOutput, calls=%fused_computation.15 | convolution fusion | flops 1509949440 | bytes 7667712 | tf_op jit(solution)/shard_map/dot_general | solution.py:373
  103.3 4.6 %fusion.3 = f32[320,3072]{1,0:T(8,128)S(1)} fusion(bf16[1,768,3072]{2,1,0:T(8,128)(2,1)} %param.26, f32[320,768]{1,0:T(8,128)S(1)} %fusion.5, f32[320,768]{1,0:T(8,128)S(1)} %fusion.13, f32[320,768]{1,0:T(8,128)S(1)} %copy-done.16), kind=kOutput, calls=%fused_computation.5 | convolution fusion | flops 1512407040 | bytes 11599872 | tf_op jit(solution)/shard_map/dot_general | solution.py:508
  108.0 1.8 fusion.18
  109.9 34.9 %combine_4.1 = (f32[128,384]{1,0:T(8,128)S(1)}, f32[8,128]{1,0:T(8,128)S(1)}) custom-call(bf16[4,80,3072]{2,1,0:T(8,128)(2,1)S(1)} %bitcast.143, bf16[4,4,128,80]{3,2,1,0:T(8,128)(2,1)S(1)} %copy.105.picks_ref, bf16[128,384]{1,0:T(8,128)(2,1)S(1)} %copy-done.1, f32[1,384]{1,0:T(1,128)S(1)} %broadcast_in_dim.38.gain_ref), custom_call_target="tpu_custom_call" | custom-call | tf_op jit(solution)/shard_map/combine_4/pallas_call | solution.py:219
  145.0 1.4 convolution_convert_fusion.1.refs_0_
  146.4 0.9 reduce-scatter.2.cloned.1.call-done.refs_1_
  147.4 14.6 %exchange_7.1 = (bf16[8,128,256]{2,1,0:T(8,128)(2,1)}, bf16[8,80,384]{2,1,0:T(8,128)(2,1)}) custom-call(bf16[128,2048]{1,0:T(8,128)(2,1)} %convolution_convert_fusion.1.refs_0_, bf16[80,3072]{1,0:T(8,128)(2,1)} %reduce-scatter.2.cloned.1.call-done.refs_1_), custom_call_target="tpu_custom_call" | custom-call | tf_op jit(solution)/shard_map/exchange_7/pallas_call | solution.py:88
  162.0 1.2 convert_reduce_fusion.1
  163.5 0.8 fusion.36.refs_0_
  164.3 10.5 %exchange_8.1 = bf16[4,2,128,128]{3,2,1,0:T(8,128)(2,1)} custom-call(bf16[2,128,128]{2,1,0:T(8,128)(2,1)} %fusion.36.refs_0_), custom_call_target="tpu_custom_call" | custom-call | tf_op jit(solution)/shard_map/exchange_8/pallas_call | solution.py:88
  174.8 1.7 convert_reduce_fusion.2
  176.6 0.3 fusion.47
  176.9 0.3 convolution_bitcast_fusion.2
  177.1 0.2 fusion.32
  177.4 0.2 convolution_bitcast_fusion.4
  177.7 0.7 copy.119
  178.6 0.7 copy.118
  179.5 0.7 copy.117
  180.3 1.2 fusion.26
  (87 shorter events, 2.3 us)
Async XLA Ops:
  7.2 3.9 %copy-start = (bf16[128,256]{1,0:T(8,128)(2,1)S(1)}, bf16[128,256]{1,0:T(8,128)(2,1)}, u32[]{:S(2)}) copy-start(bf16[128,256]{1,0:T(8,128)(2,1)} %param.17) | copy-start | bytes 196612
  7.2 29.9 %copy-start.7 = (bf16[128,256]{1,0:T(8,128)(2,1)S(1)}, bf16[128,256]{1,0:T(8,128)(2,1)}, u32[]{:S(2)}) copy-start(bf16[128,256]{1,0:T(8,128)(2,1)} %param.16) | copy-start | bytes 196612
  7.2 30.4 %copy-start.10 = (f32[256]{0:T(256)S(1)}, f32[256]{0:T(256)}, u32[]{:S(2)}) copy-start(f32[256]{0:T(256)} %param.19) | copy-start | bytes 3076
  7.2 39.5 %copy-start.9 = (f32[3072]{0:T(1024)S(1)}, f32[3072]{0:T(1024)}, u32[]{:S(2)}) copy-start(f32[3072]{0:T(1024)} %param.22) | copy-start | bytes 36868
  7.2 44.2 %copy-start.8 = (bf16[128,384]{1,0:T(8,128)(2,1)S(1)}, bf16[128,384]{1,0:T(8,128)(2,1)}, u32[]{:S(2)}) copy-start(bf16[128,384]{1,0:T(8,128)(2,1)} %param.21) | copy-start | bytes 294916
  7.2 44.2 %all-gather.3.cloned.1.call-start = ((), (), s32[]{:S(2)}) async-start(), calls=%async_computation.1 | async-start | bytes 1966080 | tf_op jit(solution)/shard_map/all_gather | solution.py:411
  8.0 90.6 %all-gather.5.cloned.1.call-start = ((), (), s32[]{:S(2)}) async-start(), calls=%async_computation.2 | async-start | bytes 2457600 | tf_op jit(solution)/shard_map/all_gather | solution.py:443
  29.9 16.7 %copy-start.13 = (f32[4,8,128]{2,1,0:T(8,128)S(1)}, f32[4,8,128]{2,1,0:T(8,128)}, u32[]{:S(2)}) copy-start(f32[4,8,128]{2,1,0:T(8,128)} %get-tuple-element.15) | copy-start | bytes 49156
  33.7 113.7 %reduce-scatter.2.cloned.1.call-start = ((), (), s32[]{:S(2)}) async-start(), calls=%async_computation.3 | async-start | bytes 2457600 | tf_op jit(solution)/shard_map/reduce_scatter | solution.py:496
  76.7 2.8 %copy-start.2 = (bf16[512,3072]{1,0:T(8,128)(2,1)S(1)}, bf16[512,3072]{1,0:T(8,128)(2,1)}, u32[]{:S(2)}) copy-start(bf16[512,3072]{1,0:T(8,128)(2,1)} %spread_3.1) | copy-start | bytes 9437188
  76.7 4.7 %slice-start.2 = ((s8[4718592]{0:T(1024)(128)(4,1)}), s8[4194304]{0:T(1024)(128)(4,1)S(1)}, s32[]{:S(2)}) async-start(s8[4718592]{0:T(1024)(128)(4,1)} %bitcast.164), calls=%async_computation.6 | async-start | bytes 8388608
  79.5 1.9 %slice-start.3 = ((s8[4718592]{0:T(1024)(128)(4,1)}), s8[524288]{0:T(1024)(128)(4,1)S(1)}, s32[]{:S(2)}) async-start(s8[4718592]{0:T(1024)(128)(4,1)} %bitcast.164), calls=%async_computation.7 | async-start | bytes 1048576
  80.7 2.5 %slice-start.4 = ((s8[4718592]{0:T(1024)(128)(4,1)}), s8[4194304]{0:T(1024)(128)(4,1)S(1)}, s32[]{:S(2)}) async-start(s8[4718592]{0:T(1024)(128)(4,1)} %bitcast.166), calls=%async_computation.8 | async-start | bytes 8388608
  81.5 1.8 slice-start.5
  81.5 4.6 %slice-start = ((s8[4718592]{0:T(1024)(128)(4,1)}), s8[4194304]{0:T(1024)(128)(4,1)S(1)}, s32[]{:S(2)}) async-start(s8[4718592]{0:T(1024)(128)(4,1)} %bitcast.162), calls=%async_computation.4 | async-start | bytes 8388608
  83.3 2.8 %slice-start.1 = ((s8[4718592]{0:T(1024)(128)(4,1)}), s8[524288]{0:T(1024)(128)(4,1)S(1)}, s32[]{:S(2)}) async-start(s8[4718592]{0:T(1024)(128)(4,1)} %bitcast.162), calls=%async_computation.5 | async-start | bytes 1048576
  85.1 1.0 copy-start.15
  86.1 3.8 %copy-start.12 = (s32[128,2]{0,1:T(2,128)S(1)}, s32[128,2]{0,1:T(2,128)}, u32[]{:S(2)}) copy-start(s32[128,2]{0,1:T(2,128)} %param.23) | copy-start | bytes 3076
  86.1 3.9 %copy-start.14 = (s32[128,2]{0,1:T(2,128)S(1)}, s32[128,2]{0,1:T(2,128)}, u32[]{:S(2)}) copy-start(s32[128,2]{0,1:T(2,128)} %param.24) | copy-start | bytes 3076
  86.1 3.9 %copy-start.11 = (f32[128,2]{0,1:T(2,128)S(1)}, f32[128,2]{0,1:T(2,128)}, u32[]{:S(2)}) copy-start(f32[128,2]{0,1:T(2,128)} %param.25) | copy-start | bytes 3076
  98.5 4.8 %copy-start.16 = (f32[320,768]{1,0:T(8,128)S(1)}, f32[320,768]{1,0:T(8,128)}, u32[]{:S(2)}) copy-start(f32[320,768]{1,0:T(8,128)} %copy-done.15) | copy-start | bytes 2949124
  98.5 9.5 %slice-start.6 = ((s8[4718592]{0:T(1024)(128)(4,1)}), s8[4194304]{0:T(1024)(128)(4,1)S(1)}, s32[]{:S(2)}) async-start(s8[4718592]{0:T(1024)(128)(4,1)} %bitcast.168), calls=%async_computation.10 | async-start | bytes 8388608
  103.3 4.7 %slice-start.7 = ((s8[4718592]{0:T(1024)(128)(4,1)}), s8[524288]{0:T(1024)(128)(4,1)S(1)}, s32[]{:S(2)}) async-start(s8[4718592]{0:T(1024)(128)(4,1)} %bitcast.168), calls=%async_computation.11 | async-start | bytes 1048576
  108.0 1.9 %copy-start.1 = (bf16[128,384]{1,0:T(8,128)(2,1)S(1)}, bf16[128,384]{1,0:T(8,128)(2,1)}, u32[]{:S(2)}) copy-start(bf16[128,384]{1,0:T(8,128)(2,1)} %fusion.27.block_ref.stream_ref) | copy-start | bytes 294916
  108.0 36.8 %copy-start.6 = (bf16[128,384]{1,0:T(8,128)(2,1)S(1)}, bf16[128,384]{1,0:T(8,128)(2,1)}, u32[]{:S(2)}) copy-start(bf16[128,384]{1,0:T(8,128)(2,1)} %refs_2_.1) | copy-start | bytes 294916
  108.0 37.0 %copy-start.3 = (bf16[2048,384]{1,0:T(8,128)(2,1)S(1)}, bf16[2048,384]{1,0:T(8,128)(2,1)}, u32[]{:S(2)}) copy-start(bf16[2048,384]{1,0:T(8,128)(2,1)} %all-gather.3.cloned.1.call-done) | copy-start | bytes 4718596
  145.0 34.4 %copy-start.5 = (bf16[128,384]{1,0:T(8,128)(2,1)}, bf16[128,384]{1,0:T(8,128)(2,1)S(1)}, u32[]{:S(2)}) copy-start(bf16[128,384]{1,0:T(8,128)(2,1)S(1)} %fusion.44) | copy-start | bytes 294916
  162.0 18.3 %copy-start.4 = (bf16[8,80,384]{2,1,0:T(8,128)(2,1)S(1)}, bf16[8,80,384]{2,1,0:T(8,128)(2,1)}, u32[]{:S(2)}) copy-start(bf16[8,80,384]{2,1,0:T(8,128)(2,1)} %get-tuple-element.18) | copy-start | bytes 1474564
Sparse Core Ops, SparseCore 0:
  9.6 41.7 all-gather.2
  53.0 45.5 all-gather.4
  100.8 46.4 reduce-scatter.1

commit v3 on v2

--- a/solution.py
+++ b/solution.py
@@ -245,6 +245,110 @@
     )(rows, picks, stream, gain)
 
 
+def dims(left, right):
+    return (((left,), (right,)), ((), ()))
+
+
+def dot32(left, right, contract):
+    return lax.dot_general(left, right, contract, preferred_element_type=jnp.float32)
+
+
+def dot_high(left, right, contract):
+    return lax.dot_general(
+        left.astype(jnp.float32),
+        right,
+        contract,
+        precision=lax.Precision.HIGHEST,
+        preferred_element_type=jnp.float32,
+    )
+
+
+def masked(scores):
+    rows = lax.broadcasted_iota(jnp.int32, scores.shape, 0)
+    cols = lax.broadcasted_iota(jnp.int32, scores.shape, 1)
+    return jnp.where(rows >= cols, scores, 0.0).astype(jnp.bfloat16)
+
+
+def head_slices(state_ref):
+    heads, size = state_ref.shape[-3], state_ref.shape[-1]
+    return [(head, slice(head * size, (head + 1) * size)) for head in range(heads)]
+
+
+def attend_kernel(
+    query_ref, key_ref, value_ref, init_ref, kv_ref, gain_ref, attended_ref, normed_ref, prefix_ref
+):
+    mine = lax.axis_index("ctx")
+    for head, part in head_slices(init_ref):
+        prefix = init_ref[head]
+        for block in range(kv_ref.shape[0]):
+            prefix += jnp.where(block < mine, kv_ref[block, head].astype(jnp.float32), 0.0)
+        prefix_ref[head] = prefix
+        query = query_ref[:, part]
+        scores = masked(dot32(query, key_ref[:, part], dims(1, 1)))
+        attended = dot_high(query, prefix, dims(1, 0)) + dot32(
+            scores, value_ref[:, part], dims(1, 0)
+        )
+        attended_ref[:, part] = attended
+        normed_ref[:, part] = head_normalize(attended, gain_ref[:, part]).astype(jnp.bfloat16)
+
+
+def pull_kernel(terms_ref, attended_ref, gain_ref, query_ref, grad_ref, state_ref):
+    for head, part in head_slices(state_ref):
+        grad_heads = terms_ref[0, :, part].astype(jnp.float32)
+        for place in range(1, terms_ref.shape[0]):
+            grad_heads += terms_ref[place, :, part].astype(jnp.float32)
+        attended = attended_ref[:, part]
+        scaled = grad_heads * gain_ref[:, part]
+        factor = lax.rsqrt(jnp.mean(attended * attended, -1, keepdims=True) + 1e-06)
+        inner = jnp.mean(attended * scaled, -1, keepdims=True)
+        grad = (factor * scaled - attended * (factor * factor * factor * inner)).astype(
+            jnp.bfloat16
+        )
+        grad_ref[:, part] = grad
+        state_ref[head] = dot32(query_ref[:, part], grad, dims(0, 0)).astype(jnp.bfloat16)
+
+
+def finish_kernel(
+    query_ref, key_ref, value_ref, grad_ref, prefix_ref, states_ref,
+    grad_query_ref, grad_key_ref, grad_value_ref, total_ref,
+):
+    mine = lax.axis_index("ctx")
+    for head, part in head_slices(prefix_ref):
+        later = jnp.zeros(prefix_ref.shape[1:], jnp.float32)
+        total = later
+        for block in range(states_ref.shape[0]):
+            state = states_ref[block, head].astype(jnp.float32)
+            total += state
+            later += jnp.where(block > mine, state, 0.0)
+        total_ref[head] = total
+        query, key, value, grad = (
+            query_ref[:, part], key_ref[:, part], value_ref[:, part], grad_ref[:, part]
+        )
+        scores = masked(dot32(query, key, dims(1, 1)))
+        grad_scores = masked(dot32(grad, value, dims(1, 1)))
+        grad_query_ref[:, part] = (
+            dot_high(grad, prefix_ref[head], dims(1, 1)) + dot32(grad_scores, key, dims(1, 0))
+        ).astype(jnp.bfloat16)
+        grad_key_ref[:, part] = (
+            dot_high(value, later, dims(1, 1)) + dot32(grad_scores, query, dims(0, 0))
+        ).astype(jnp.bfloat16)
+        grad_value_ref[:, part] = (
+            dot_high(key, later, dims(1, 0)) + dot32(scores, grad, dims(0, 0))
+        ).astype(jnp.bfloat16)
+
+
+def on_device(kernel, outputs, name, *operands):
+    vmem = pl.BlockSpec(memory_space=pltpu.VMEM)
+    return pl.pallas_call(
+        kernel,
+        out_shape=[jax.ShapeDtypeStruct(shape, kind) for shape, kind in outputs],
+        in_specs=[vmem] * len(operands),
+        out_specs=[vmem] * len(outputs),
+        compiler_params=pltpu.CompilerParams(vmem_limit_bytes=24 * 1024 * 1024),
+        name=name,
+    )(*operands)
+
+
 def spread_kernel(block_ref, all_ref, z_send, z_recv, xy_send, xy_recv, pair_send, pair_recv, own_sem):
     rows, width = block_ref.shape
     blocks = lax.axis_size("ctx")
@@ -409,10 +513,16 @@
     capacity = 5 * tokens_here // (2 * expert_count)
     slots_all = ctx_count * capacity
     w_cols = lax.all_gather(out_weight, "ctx", axis=0, tiled=True)
-    query3 = query_act.reshape(tokens_here, head_count, head_size)
-    key3 = key_act.reshape(tokens_here, head_count, head_size)
-    value3 = value_act.reshape(tokens_here, head_count, head_size)
-    kv_own = jnp.einsum("thd,the->hde", key3, value3, preferred_element_type=f32)
+    kv_own = jnp.stack(
+        [
+            dot32(
+                key_act[:, head * head_size : (head + 1) * head_size],
+                value_act[:, head * head_size : (head + 1) * head_size],
+                dims(0, 0),
+            )
+            for head in range(head_count)
+        ]
+    )
     meta = jnp.concatenate(
         [expert_ids.T.astype(f32), expert_slots.T.astype(f32), route_gates.T, route_gates.T], 0
     )
@@ -443,17 +553,18 @@
     grad_rows = lax.all_gather(
         (grad_own * here_gates[:, None]).astype(bf16), "ctx", axis=0, tiled=True
     )
-    earlier = (jnp.arange(ctx_count) < my_ctx).astype(f32)
-    prefix = state_init + jnp.sum(earlier[:, None, None, None] * kv_all.astype(f32), 0)
-    causal = jnp.arange(tokens_here)[:, None] >= jnp.arange(tokens_here)[None, :]
-    scores = jnp.einsum("thd,shd->hts", query3, key3, preferred_element_type=f32)
-    scores_bf = jnp.where(causal[None], scores, 0.0).astype(bf16)
-    inside = jnp.einsum("hts,she->the", scores_bf, value3, preferred_element_type=f32)
-    from_state = jnp.einsum("thd,hde->the", query3.astype(f32), prefix, precision=high)
-    attended = from_state + inside
-    gain_heads = head_gain.reshape(head_count, head_size)
-    normed_heads = (
-        head_normalize(attended, gain_heads).astype(bf16).reshape(tokens_here, heads_width)
+    flat_shape = (tokens_here, heads_width)
+    gain_row = head_gain[None]
+    attended, normed_heads, prefix = on_device(
+        attend_kernel,
+        [(flat_shape, f32), (flat_shape, bf16), (state_init.shape, f32)],
+        "attend",
+        query_act,
+        key_act,
+        value_act,
+        state_init,
+        kv_all,
+        gain_row,
     )
     normed_all = exchange(
         "ep",
@@ -550,16 +661,29 @@
         - stream_f * row_scale**3 * inner_sum[:, None] / model_width
     ).astype(bf16)
     head_parts = contract_last(grad_stream, w_cols).astype(bf16)
-    out_parts, out_of = column_parts(half_out, ep_count)
-    head_terms, returned = exchange(
+    head_terms = exchange(
         "ep",
         7,
+        [(head_parts, lanes(heads_width), (ep_count, tokens_here, heads_width), leading)],
+    )[0]
+    grad_attended, state_part = on_device(
+        pull_kernel,
+        [(flat_shape, bf16), (state_init.shape, bf16)],
+        "pull",
+        head_terms,
+        attended,
+        gain_row,
+        query_act,
+    )
+    out_parts, out_of = column_parts(half_out, ep_count)
+    state_all, returned = exchange(
+        "ctx",
+        8,
         [
-            (head_parts, lanes(heads_width), (ep_count, tokens_here, heads_width), leading),
-            (out_parts, out_of, (ep_count, capacity, columns), leading),
+            (state_part, whole_ref, (ctx_count,) + state_part.shape, leading),
+            (out_parts, out_of, (ep_count, capacity, columns), leading, "ep"),
         ],
     )
-    grad_heads = jnp.sum(head_terms.astype(f32), 0)
     local_hits = (expert_ids[:, :, None, None] == (jnp.arange(ep_count) % expert_count)[:, None]) & (
         expert_slots[:, :, None, None] == jnp.arange(capacity)
     )
@@ -570,38 +694,18 @@
         dest_weights, returned.reshape(ep_count * capacity, columns).astype(f32), precision=high
     )
     layer_out = (stream_f + expert_mix).astype(bf16)
-    head_pull = jax.vjp(lambda value: head_normalize(value, gain_heads), attended)[1]
-    grad_attended = head_pull(grad_heads.reshape(tokens_here, head_count, head_size))[0].astype(
-        bf16
-    )
-    state_part = jnp.einsum("thd,the->hde", query3, grad_attended, preferred_element_type=f32)
-    state_all = exchange(
-        "ctx", 8, [(state_part.astype(bf16), whole_ref, (ctx_count,) + state_part.shape, leading)]
-    )[0].astype(f32)
-    after = (jnp.arange(ctx_count) > my_ctx).astype(f32)
-    later_sum = jnp.sum(after[:, None, None, None] * state_all, 0)
-    state_total = jnp.sum(state_all, 0)
-    grad_scores = jnp.einsum("the,she->hts", grad_attended, value3, preferred_element_type=f32)
-    grad_masked = jnp.where(causal[None], grad_scores, 0.0).astype(jnp.bfloat16)
-    grad_att_f = grad_attended.astype(f32)
-    grad_query = jnp.einsum("the,hde->thd", grad_att_f, prefix, precision=high) + jnp.einsum(
-        "hts,shd->thd", grad_masked, key3, preferred_element_type=f32
-    )
-    grad_key = jnp.einsum(
-        "the,hde->thd", value3.astype(f32), later_sum, precision=high
-    ) + jnp.einsum("hts,thd->shd", grad_masked, query3, preferred_element_type=f32)
-    grad_value = jnp.einsum(
-        "thd,hde->the", key3.astype(f32), later_sum, precision=high
-    ) + jnp.einsum("hts,the->she", scores_bf, grad_attended, preferred_element_type=f32)
-    flat_shape = (tokens_here, head_count * head_size)
-    return (
-        layer_out,
-        grad_query.astype(jnp.bfloat16).reshape(flat_shape),
-        grad_key.astype(jnp.bfloat16).reshape(flat_shape),
-        grad_value.astype(jnp.bfloat16).reshape(flat_shape),
-        state_total,
-        grad_stream,
-    )
+    grad_query, grad_key, grad_value, state_total = on_device(
+        finish_kernel,
+        [(flat_shape, bf16), (flat_shape, bf16), (flat_shape, bf16), (state_init.shape, f32)],
+        "finish",
+        query_act,
+        key_act,
+        value_act,
+        grad_attended,
+        prefix,
+        state_all,
+    )
+    return layer_out, grad_query, grad_key, grad_value, state_total, grad_stream
 
 
 def solution(mesh):

time: 188 us -> 184 us (0.979)
  waiting for transfers between devices: 14.4 us -> 7.32 us
  other arithmetic: 13.7 us -> 9.77 us
  local copies, waits for them, and re-layouts: 6.51 us -> 9.71 us
  Pallas kernels: 109 us -> 112 us
    unnamed x53 -> x64, local copies, waits for them, and re-layouts: 3.4 us -> 8.5 us
    all_gather x1, waiting for transfers between devices: 4.45 us -> 0.02 us  [local(): w_cols = lax.all_gather(out_weight, 'ctx', axis=0, tiled=True)]
    reduce_sum x4 -> x0, other arithmetic: 4.13 us -> none  [the longest x1 1.74 us: local(): state_total = jnp.sum(state_all, 0)]
    pallas_call x1, Pallas kernels: 22.7 us -> 25.9 us  [spread(): pl.pallas_call(spread_kernel, out_shape=jax.ShapeDtypeStruct((blocks * ro...]
    pallas_call x4, Pallas kernels: 51.5 us -> 48.6 us  [exchange(): pl.pallas_call(functools.partial(exchange_kernel, axes, [item[1] for item...]
    reshape x3 -> x0, local copies, waits for them, and re-layouts: 2.65 us -> none  [the longest x1 0.95 us: local(): query3 = query_act.reshape(tokens_here, head_count, head_size)]
    pallas_call x0 -> x3, Pallas kernels: none -> 2.49 us  [on_device(): pl.pallas_call(kernel, out_shape=[jax.ShapeDtypeStruct(shape, kind) for s...]
    dot_general x12 -> x2, matrix products: 3.77 us -> 1.91 us  [dot32(): lax.dot_general(left, right, contract, preferred_element_type=jnp.float32)]
  transfers between devices with their start and end apart: 3 -> 3, of which waited for: 3 -> 1; matrix products, arithmetic and copies ran while one was open for 21% -> 21% of each run, Pallas kernels for 45% -> 54%
where the time goes in v3:
time: 184 us; the launch traced here: 183 us
  Pallas kernels  112 us (61%)
  matrix products  29.2 us (16%)
  between operations  14.3 us (8%)
  other arithmetic  9.77 us (5%)
  local copies, waits for them, and re-layouts  9.71 us (5%)
  waiting for transfers between devices  7.32 us (4%)
    pallas_call x4, Pallas kernels, exchange(): pl.pallas_call(functools.partial(exchange_kernel, axes, [item[1] for item...  48.6 us
    pallas_call x1, Pallas kernels, combine(): pl.pallas_call(combine_kernel, out_shape=[jax.ShapeDtypeStruct((tokens, w...  35.5 us
    pallas_call x1, Pallas kernels, spread(): pl.pallas_call(spread_kernel, out_shape=jax.ShapeDtypeStruct((blocks * ro...  25.9 us
    dot_general x4, matrix products, contract_last(): lax.dot_general(left, right, (((1,), (1,)), ((), ())), preferred_element_...  9.85 us
    unnamed x64, local copies, waits for them, and re-layouts  8.5 us
    all_gather x1, waiting for transfers between devices, local(): lax.all_gather((grad_own * here_gates[:, None]).astype(bf16), 'ctx', axis...  6.59 us
    dot_general x1, matrix products, local(): jnp.dot(grad_gate_pre, w_gate, preferred_element_type=f32)  4.6 us
  transfers between devices with their start and end apart: 3, of which 1 were waited for; matrix products, arithmetic and copies ran while one was open for 21% of the time, Pallas kernels for 54%

profile of v3, /device:TPU:0, one launch (start us, length us, event | category | flops | bytes accessed | tf_op | source)
XLA Modules:
  0.0 182.8 jit_solution(8034767426849957058)
XLA Ops:
  7.2 0.7 all-gather.3.cloned.1.call-update
  8.0 0.7 convert_bitcast_fusion
  8.7 1.4 pad_maximum_fusion.1.refs_1_
  10.0 1.0 fusion.28
  11.0 1.0 fusion.29
  12.0 0.6 pad_maximum_fusion.refs_0_
  12.6 19.7 %exchange_1.1 = (bf16[4,2,128,128]{3,2,1,0:T(8,128)(2,1)}, f32[4,8,128]{2,1,0:T(8,128)}, bf16[128,3072]{1,0:T(8,128)(2,1)}) custom-call(bf16[2,128,128]{2,1,0:T(8,128)(2,1)} %pad_maximum_fusion.refs_0_, f32[8,128]{1,0:T(8,128)} %pad_maximum_fusion.1.refs_1_, bf16[128,384]{1,0:T(8,128)(2,1)} %refs_2_.1), custom_call_target="tpu_custom_call" | custom-call | tf_op jit(solution)/shard_map/exchange_1/pallas_call | solution.py:88
  32.3 0.7 broadcast_compare_fusion.4
  33.0 0.8 convert_reduce_fusion.2
  33.8 2.2 %fusion.24 = bf16[80,3072]{1,0:T(8,128)(2,1)} fusion(bf16[128,3072]{1,0:T(8,128)(2,1)} %get-tuple-element.24, f32[80]{0:T(128)S(1)} %get-tuple-element.39, bf16[128,80]{0,1:T(8,128)(2,1)S(1)} %get-tuple-element.38), kind=kOutput, calls=%fused_computation.22 | convolution fusion | flops 63406080 | bytes 1298752 | tf_op jit(solution)/shard_map/dot_general | solution.py:550
  36.1 0.8 fusion.47
  36.9 0.7 broadcast_compare_fusion.3
  37.6 0.8 copy-done.2
  38.5 0.8 copy-done.4
  39.3 0.8 copy-done.6
  40.1 0.9 copy-done.8
  41.1 0.9 copy-done.10
  42.0 0.7 copy-done.13
  42.7 0.6 attend.1
  43.3 0.6 copy-done.12
  43.9 8.2 %exchange_2.1 = bf16[128,2048]{1,0:T(8,128)(2,1)} custom-call(bf16[128,256]{1,0:T(8,128)(2,1)} %copy-done.12), custom_call_target="tpu_custom_call" | custom-call | tf_op jit(solution)/shard_map/exchange_2/pallas_call | solution.py:88
  52.3 0.1 convert_reduce_fusion.1
  52.4 2.7 %fusion.27.block_ref.stream_ref = bf16[128,384]{1,0:T(8,128)(2,1)} fusion(bf16[128,2048]{1,0:T(8,128)(2,1)} %exchange_2.1, bf16[2048,384]{1,0:T(8,128)(2,1)} %all-gather.3.cloned.1.call-done, bf16[128,384]{1,0:T(8,128)(2,1)S(1)} %copy-done.19), kind=kOutput, calls=%fused_computation.29 | convolution fusion | flops 201474048 | bytes 2293760 | tf_op jit(solution)/shard_map/dot_general | solution.py:574
  55.1 25.9 %spread_3.1 = bf16[512,3072]{1,0:T(8,128)(2,1)} custom-call(bf16[128,384]{1,0:T(8,128)(2,1)} %fusion.27.block_ref.stream_ref), custom_call_target="tpu_custom_call" | custom-call | tf_op jit(solution)/shard_map/spread_3/pallas_call | solution.py:453
  81.0 2.7 %fusion = f32[512]{0:T(512)S(1)} fusion(bf16[512,3072]{1,0:T(8,128)(2,1)} %spread_3.1), kind=kLoop, calls=%fused_computation.2 | loop fusion | flops 4718080 | bytes 3147776 | tf_op jit(solution)/shard_map/reduce_sum | solution.py:579
  83.9 1.2 fusion.2
  85.1 0.7 convolution_convert_fusion
  85.8 1.8 fusion.5
  87.7 1.8 fusion.9
  89.6 3.1 %fusion.21 = bf16[320,3072]{1,0:T(8,128)(2,1)} fusion(bf16[1,768,3072]{2,1,0:T(8,128)(2,1)S(1)} %bitcast.67, f32[320,768]{1,0:T(8,128)S(1)} %fusion.9, f32[320,768]{1,0:T(8,128)S(1)} %fusion.5), kind=kOutput, calls=%fused_computation.19 | convolution fusion | flops 1512407040 | bytes 8650752 | tf_op jit(solution)/shard_map/dot_general | solution.py:608
  92.7 0.1 broadcast_compare_fusion
  92.8 0.2 convert_reduce_fusion
  93.0 0.3 copy.27.picks_ref
  93.7 6.6 %all-gather.5.cloned.1.call-done = bf16[320,3072]{1,0:T(8,128)(2,1)} async-done(((bf16[80,3072]{1,0:T(8,128)(2,1)}), bf16[320,3072]{1,0:T(8,128)(2,1)}) %all-gather.5.cloned.1.call-update) | async-done | bytes 1966096 | tf_op jit(solution)/shard_map/all_gather | solution.py:553
  100.3 4.8 %fusion.13 = f32[320,768]{1,0:T(8,128)S(1)} fusion(bf16[320,3072]{1,0:T(8,128)(2,1)} %all-gather.5.cloned.1.call-done, bf16[1,768,3072]{2,1,0:T(8,128)(2,1)} %param.28), kind=kOutput, calls=%fused_computation.15 | convolution fusion | flops 1509949440 | bytes 7667712 | tf_op jit(solution)/shard_map/dot_general | solution.py:477
  105.1 4.6 %fusion.3 = f32[320,3072]{1,0:T(8,128)S(1)} fusion(bf16[1,768,3072]{2,1,0:T(8,128)(2,1)} %param.26, f32[320,768]{1,0:T(8,128)S(1)} %fusion.5, f32[320,768]{1,0:T(8,128)S(1)} %fusion.13, f32[320,768]{1,0:T(8,128)S(1)} %fusion.9), kind=kOutput, calls=%fused_computation.5 | convolution fusion | flops 1512407040 | bytes 11599872 | tf_op jit(solution)/shard_map/dot_general | solution.py:619
  109.7 1.9 %fusion.18 = bf16[320,3072]{1,0:T(8,128)(2,1)S(1)} fusion(f32[320,3072]{1,0:T(8,128)S(1)} %fusion.3, bf16[1,768,3072]{2,1,0:T(8,128)(2,1)S(1)} %bitcast.73, f32[320,768]{1,0:T(8,128)S(1)} %fusion.13, f32[320,768]{1,0:T(8,128)S(1)} %fusion.5), kind=kOutput, calls=%fused_computation.18 | convolution fusion | flops 1513390080 | bytes 12582912 | tf_op jit(solution)/shard_map/dot_general | solution.py:620
  111.8 35.5 %combine_4.1 = (f32[128,384]{1,0:T(8,128)S(1)}, f32[8,128]{1,0:T(8,128)S(1)}) custom-call(bf16[4,80,3072]{2,1,0:T(8,128)(2,1)S(1)} %bitcast.59, bf16[4,4,128,80]{3,2,1,0:T(8,128)(2,1)S(1)} %copy.27.picks_ref, bf16[128,384]{1,0:T(8,128)(2,1)S(1)} %copy-done, f32[1,384]{1,0:T(1,128)S(1)} %broadcast_in_dim.19.gain_ref), custom_call_target="tpu_custom_call" | custom-call | tf_op jit(solution)/shard_map/combine_4/pallas_call | solution.py:219
  147.3 0.1 fusion.36
  147.4 1.4 convolution_convert_fusion.1.refs_0_
  148.9 9.0 %exchange_7.1.terms_ref = bf16[8,128,256]{2,1,0:T(8,128)(2,1)} custom-call(bf16[128,2048]{1,0:T(8,128)(2,1)} %convolution_convert_fusion.1.refs_0_), custom_call_target="tpu_custom_call" | custom-call | tf_op jit(solution)/shard_map/exchange_7/pallas_call | solution.py:88
  157.9 1.0 copy-done.1
  158.9 0.3 pull.1
  159.2 0.6 copy-done.11
  159.8 11.7 %exchange_8.1 = (bf16[4,2,128,128]{3,2,1,0:T(8,128)(2,1)}, bf16[8,80,384]{2,1,0:T(8,128)(2,1)}) custom-call(bf16[2,128,128]{2,1,0:T(8,128)(2,1)} %copy-done.11, bf16[80,3072]{1,0:T(8,128)(2,1)} %reduce-scatter.2.cloned.1.call-done.refs_1_), custom_call_target="tpu_custom_call" | custom-call | tf_op jit(solution)/shard_map/exchange_8/pallas_call | solution.py:88
  171.6 2.2 %fusion.26 = bf16[128,384]{1,0:T(8,128)(2,1)} fusion(f32[128,8,80]{0,2,1:T(8,128)S(1)} %select_reduce_fusion, bf16[8,80,384]{2,1,0:T(8,128)(2,1)} %get-tuple-element.30, bf16[128,384]{1,0:T(8,128)(2,1)S(1)} %copy-done), kind=kOutput, calls=%fused_computation.28 | convolution fusion | flops 377634816 | bytes 1015808 | tf_op jit(solution)/shard_map/dot_general | solution.py:693
  173.8 0.9 copy-done.9
  174.7 1.6 finish.1
  (77 shorter events, 0.9 us)
Async XLA Ops:
  7.2 45.0 %copy-start.20 = (f32[3072]{0:T(1024)S(1)}, f32[3072]{0:T(1024)}, u32[]{:S(2)}) copy-start(f32[3072]{0:T(1024)} %param.22) | copy-start | bytes 36868
  7.2 45.3 %copy-start.19 = (bf16[128,384]{1,0:T(8,128)(2,1)S(1)}, bf16[128,384]{1,0:T(8,128)(2,1)}, u32[]{:S(2)}) copy-start(bf16[128,384]{1,0:T(8,128)(2,1)} %param.21) | copy-start | bytes 294916
  7.2 45.2 %all-gather.3.cloned.1.call-start = ((), (), s32[]{:S(2)}) async-start(), calls=%async_computation.1 | async-start | bytes 1966080 | tf_op jit(solution)/shard_map/all_gather | solution.py:515
  7.9 92.3 %all-gather.5.cloned.1.call-start = ((), (), s32[]{:S(2)}) async-start(), calls=%async_computation.2 | async-start | bytes 2457600 | tf_op jit(solution)/shard_map/all_gather | solution.py:553
  36.0 123.8 %reduce-scatter.2.cloned.1.call-start = ((), (), s32[]{:S(2)}) async-start(), calls=%async_computation.3 | async-start | bytes 2457600 | tf_op jit(solution)/shard_map/reduce_scatter | solution.py:607
  37.6 0.8 copy-start.2
  38.5 0.8 copy-start.4
  39.3 0.8 copy-start.6
  40.1 0.9 copy-start.8
  41.1 0.9 copy-start.10
  42.0 0.7 copy-start.13
  43.3 0.6 copy-start.12
  81.0 2.8 %copy-start.15 = (bf16[512,3072]{1,0:T(8,128)(2,1)S(1)}, bf16[512,3072]{1,0:T(8,128)(2,1)}, u32[]{:S(2)}) copy-start(bf16[512,3072]{1,0:T(8,128)(2,1)} %spread_3.1) | copy-start | bytes 9437188
  81.0 4.8 %slice-start.2 = ((s8[4718592]{0:T(1024)(128)(4,1)}), s8[4194304]{0:T(1024)(128)(4,1)S(1)}, s32[]{:S(2)}) async-start(s8[4718592]{0:T(1024)(128)(4,1)} %bitcast.68), calls=%async_computation.6 | async-start | bytes 8388608
  83.8 1.9 %slice-start.3 = ((s8[4718592]{0:T(1024)(128)(4,1)}), s8[524288]{0:T(1024)(128)(4,1)S(1)}, s32[]{:S(2)}) async-start(s8[4718592]{0:T(1024)(128)(4,1)} %bitcast.68), calls=%async_computation.7 | async-start | bytes 1048576
  85.1 2.6 %slice-start.4 = ((s8[4718592]{0:T(1024)(128)(4,1)}), s8[4194304]{0:T(1024)(128)(4,1)S(1)}, s32[]{:S(2)}) async-start(s8[4718592]{0:T(1024)(128)(4,1)} %bitcast.70), calls=%async_computation.8 | async-start | bytes 8388608
  85.8 1.8 %slice-start.5 = ((s8[4718592]{0:T(1024)(128)(4,1)}), s8[524288]{0:T(1024)(128)(4,1)S(1)}, s32[]{:S(2)}) async-start(s8[4718592]{0:T(1024)(128)(4,1)} %bitcast.70), calls=%async_computation.9 | async-start | bytes 1048576
  85.8 3.7 %slice-start = ((s8[4718592]{0:T(1024)(128)(4,1)}), s8[4194304]{0:T(1024)(128)(4,1)S(1)}, s32[]{:S(2)}) async-start(s8[4718592]{0:T(1024)(128)(4,1)} %bitcast.66), calls=%async_computation.4 | async-start | bytes 8388608
  87.7 1.8 %slice-start.1 = ((s8[4718592]{0:T(1024)(128)(4,1)}), s8[524288]{0:T(1024)(128)(4,1)S(1)}, s32[]{:S(2)}) async-start(s8[4718592]{0:T(1024)(128)(4,1)} %bitcast.66), calls=%async_computation.5 | async-start | bytes 1048576
  89.5 3.8 %copy-start.22 = (s32[128,2]{0,1:T(2,128)S(1)}, s32[128,2]{0,1:T(2,128)}, u32[]{:S(2)}) copy-start(s32[128,2]{0,1:T(2,128)} %param.23) | copy-start | bytes 3076
  89.5 3.9 %copy-start.23 = (s32[128,2]{0,1:T(2,128)S(1)}, s32[128,2]{0,1:T(2,128)}, u32[]{:S(2)}) copy-start(s32[128,2]{0,1:T(2,128)} %param.24) | copy-start | bytes 3076
  89.5 3.9 %copy-start.21 = (f32[128,2]{0,1:T(2,128)S(1)}, f32[128,2]{0,1:T(2,128)}, u32[]{:S(2)}) copy-start(f32[128,2]{0,1:T(2,128)} %param.25) | copy-start | bytes 3076
  100.3 9.4 %slice-start.6 = ((s8[4718592]{0:T(1024)(128)(4,1)}), s8[4194304]{0:T(1024)(128)(4,1)S(1)}, s32[]{:S(2)}) async-start(s8[4718592]{0:T(1024)(128)(4,1)} %bitcast.72), calls=%async_computation.10 | async-start | bytes 8388608
  105.1 4.6 %slice-start.7 = ((s8[4718592]{0:T(1024)(128)(4,1)}), s8[524288]{0:T(1024)(128)(4,1)S(1)}, s32[]{:S(2)}) async-start(s8[4718592]{0:T(1024)(128)(4,1)} %bitcast.72), calls=%async_computation.11 | async-start | bytes 1048576
  109.7 2.0 %copy-start = (bf16[128,384]{1,0:T(8,128)(2,1)S(1)}, bf16[128,384]{1,0:T(8,128)(2,1)}, u32[]{:S(2)}) copy-start(bf16[128,384]{1,0:T(8,128)(2,1)} %fusion.27.block_ref.stream_ref) | copy-start | bytes 294916
  109.7 37.5 %copy-start.18 = (bf16[128,384]{1,0:T(8,128)(2,1)S(1)}, bf16[128,384]{1,0:T(8,128)(2,1)}, u32[]{:S(2)}) copy-start(bf16[128,384]{1,0:T(8,128)(2,1)} %refs_2_.1) | copy-start | bytes 294916
  109.7 37.7 %copy-start.16 = (bf16[2048,384]{1,0:T(8,128)(2,1)S(1)}, bf16[2048,384]{1,0:T(8,128)(2,1)}, u32[]{:S(2)}) copy-start(bf16[2048,384]{1,0:T(8,128)(2,1)} %all-gather.3.cloned.1.call-done) | copy-start | bytes 4718596
  111.7 46.2 %copy-start.7 = (bf16[128,256]{1,0:T(8,128)(2,1)S(1)}, bf16[128,256]{1,0:T(8,128)(2,1)}, u32[]{:S(2)}) copy-start(bf16[128,256]{1,0:T(8,128)(2,1)} %query_ref.5) | copy-start | bytes 196612
  111.7 46.2 %copy-start.14 = (f32[256]{0:T(256)S(1)}, f32[256]{0:T(256)}, u32[]{:S(2)}) copy-start(f32[256]{0:T(256)} %param.19) | copy-start | bytes 3076
  111.7 62.0 %copy-start.3 = (bf16[128,256]{1,0:T(8,128)(2,1)S(1)}, bf16[128,256]{1,0:T(8,128)(2,1)}, u32[]{:S(2)}) copy-start(bf16[128,256]{1,0:T(8,128)(2,1)} %key_ref.3) | copy-start | bytes 196612
  111.7 62.0 %copy-start.5 = (bf16[128,256]{1,0:T(8,128)(2,1)S(1)}, bf16[128,256]{1,0:T(8,128)(2,1)}, u32[]{:S(2)}) copy-start(bf16[128,256]{1,0:T(8,128)(2,1)} %value_ref.3) | copy-start | bytes 196612
  147.4 28.9 %copy-start.17 = (bf16[128,384]{1,0:T(8,128)(2,1)}, bf16[128,384]{1,0:T(8,128)(2,1)S(1)}, u32[]{:S(2)}) copy-start(bf16[128,384]{1,0:T(8,128)(2,1)S(1)} %fusion.36) | copy-start | bytes 294916
  157.9 1.0 copy-start.1
  159.2 0.6 copy-start.11
  173.8 1.0 copy-start.9
Sparse Core Ops, SparseCore 0:
  9.6 42.5 all-gather.2
  53.7 46.4 all-gather.4
  102.6 46.1 reduce-scatter.1
